TPU v7x, 256 devices: a whole 4x4x8 slice. The times are simulated.
256 devices in a mesh: space: 16 (over z, y_lo), replica: 16 (over x, y_hi, core).
Axes of the slice: x: 4, y: 4 (y_hi: 2, y_lo: 2; y = y_hi * 2 + y_lo), z: 8, core: 2. Of those that a mesh axis runs over, the one named last changes fastest.
Arguments:
- hologram: bfloat16 [16, 32, 64, 64, 128], P('replica', 'space'), may hold values from -6 to 6
- weight: bfloat16 [3, 3, 128, 128], replicated, may hold values from -0.1875 to 0.1875
- conv_bias: float32 [128], replicated, may hold values from -3 to 3
- cotangent: bfloat16 [16, 32, 64, 64, 128], P('replica', 'space'), may hold values from -6 to 6
- tissue: int32 [16, 32, 4096], P('replica', 'space'), may hold values 0 or 1
- owners: int32 [16, 32], P('replica'), may hold values from 0 to 31, each once within a row
- neighbours: int32 [16, 8, 32], P('replica'), may hold values from -1 to 31, as said below
Outputs:
- features: bfloat16 [16, 32, 64, 64, 128], P('replica', 'space')
- input_grad: bfloat16 [16, 32, 64, 64, 128], P('replica', 'space')
- weight_grad: float32 [3, 3, 128, 128], replicated
- bias_grad: float32 [128], replicated
Inputs may be any that keep to these rules, and one draw needn't show every extreme that they name: `owners`: each row is a permutation of the tiles; slot j lies on index j // 2 of space. `neighbours`: the tiles of a hologram stand on a grid of 64 positions, 8 to a row; entry [s, k, t] is the tile at the position next to tile t in direction k (north, south, west, east, north-west, north-east, south-west, south-east), or -1 where that position lies outside the grid or holds no tissue tile. The relation is symmetric.
All inputs are finite; a program needn't handle non-finite values. No bound on the sum of `tissue` on one device may be relied on, other than what follows from the above.
Results may differ from a plain program's by a relative error of at most 0.0075.
Values may be sent and summed in bfloat16 or wider, within the bound.
A program may use at most 64 MiB of HBM per device.

v0:
```python
import jax
import jax.numpy as jnp
from jax import lax
from jax.sharding import PartitionSpec as P


def edge_pair(tiles):
    rows = jnp.stack([tiles[:, 0], tiles[:, -1]], axis=1)
    cols = jnp.stack([tiles[:, :, 0], tiles[:, :, -1]], axis=1)
    return (rows, cols)


def neighbour_slots(owners_row, neighbours_row, my_slots):
    count = owners_row.shape[0]
    positions = jnp.arange(count, dtype=jnp.int32)
    my_tiles = jnp.sum(
        jnp.where(positions[None, :] == my_slots[:, None], owners_row[None, :], 0), axis=1
    )
    near = jnp.sum(
        jnp.where(
            positions[None, None, :] == my_tiles[None, :, None], neighbours_row[:, None, :], 0
        ),
        axis=2,
    )
    slot_of = jnp.sum(
        jnp.where(owners_row[None, None, :] == near[:, :, None], positions[None, None, :], 0),
        axis=2,
    )
    return (slot_of, near >= 0)


def assemble(tiles, rows_all, cols_all, slot_of, present):

    def face(table, direction, side):
        got = table[slot_of[direction], side]
        return jnp.where(present[direction][:, None, None], got, jnp.zeros_like(got))

    def corner(direction, side, end):
        got = rows_all[slot_of[direction], side, end]
        return jnp.where(present[direction][:, None], got, jnp.zeros_like(got))

    north = face(rows_all, 0, 1)
    south = face(rows_all, 1, 0)
    west = face(cols_all, 2, 1)
    east = face(cols_all, 3, 0)
    top = jnp.concatenate([corner(4, 1, -1)[:, None], north, corner(5, 1, 0)[:, None]], axis=1)
    bottom = jnp.concatenate([corner(6, 0, -1)[:, None], south, corner(7, 0, 0)[:, None]], axis=1)
    middle = jnp.concatenate([west[:, :, None], tiles, east[:, :, None]], axis=2)
    return jnp.concatenate([top[:, None], middle, bottom[:, None]], axis=1)


def reduce_grads(local_w, local_b):
    chan = local_b.shape[0]
    flat = local_w.reshape(-1, chan)
    flat, total_b = lax.psum((flat, local_b), ("space", "replica"))
    return (flat.reshape(local_w.shape), total_b)


def transposed_conv(grad_padded, weight):
    flipped = jnp.flip(weight, (0, 1))
    return lax.conv_general_dilated(
        grad_padded,
        flipped,
        (1, 1),
        "VALID",
        dimension_numbers=("NHWC", "HWOI", "NHWC"),
        preferred_element_type=jnp.float32,
    ).astype(jnp.bfloat16)


def local(hologram, weight, conv_bias, cotangent, tissue, owners, neighbours):
    tiles = hologram[0]
    count, height, width, chan = tiles.shape
    my_slots = lax.axis_index("space") * count + jnp.arange(count, dtype=jnp.int32)
    slot_of, present = neighbour_slots(owners[0], neighbours[0], my_slots)
    rows, cols = edge_pair(tiles)
    rows_all, cols_all = (
        lax.all_gather(rows, "space", axis=0, tiled=True),
        lax.all_gather(cols, "space", axis=0, tiled=True),
    )
    padded = assemble(tiles, rows_all, cols_all, slot_of, present)
    pre = (
        lax.conv_general_dilated(
            padded,
            weight,
            (1, 1),
            "VALID",
            dimension_numbers=("NHWC", "HWIO", "NHWC"),
            preferred_element_type=jnp.float32,
        )
        + conv_bias
    )
    keep = tissue[0].reshape(count, height, width, 1).astype(jnp.float32)
    sigma = jax.nn.sigmoid(pre)
    features = (pre * sigma * keep).astype(jnp.bfloat16)
    slope = sigma * (1.0 + pre * (1.0 - sigma))
    grad_pre = (cotangent[0].astype(jnp.float32) * keep * slope).astype(jnp.bfloat16)
    grad_rows, grad_cols = edge_pair(grad_pre)
    grad_rows_all, grad_cols_all = (
        lax.all_gather(grad_rows, "space", axis=0, tiled=True),
        lax.all_gather(grad_cols, "space", axis=0, tiled=True),
    )
    grad_padded = assemble(grad_pre, grad_rows_all, grad_cols_all, slot_of, present)
    flat_grad = grad_pre.reshape(-1, chan)
    weight_rows = []
    for row_off in range(3):
        weight_cols = []
        for col_off in range(3):
            source = padded[:, row_off : row_off + height, col_off : col_off + width].reshape(
                -1, chan
            )
            weight_cols.append(
                lax.dot_general(
                    source, flat_grad, (((0,), (0,)), ((), ())), preferred_element_type=jnp.float32
                )
            )
        weight_rows.append(jnp.stack(weight_cols))
    local_w = jnp.stack(weight_rows)
    local_b = jnp.sum(flat_grad.astype(jnp.float32), axis=0)
    input_grad = transposed_conv(grad_padded, weight)
    summed_w, summed_b = reduce_grads(local_w, local_b)
    total_cells = lax.axis_size("replica") * lax.axis_size("space") * count * height * width
    scale = float(total_cells) ** (-0.5)
    return (features[None], input_grad[None], summed_w * scale, summed_b * scale)


def solution(mesh):
    return jax.shard_map(
        local,
        mesh=mesh,
        in_specs=(
            P("replica", "space", None, None, None),
            P(),
            P(),
            P("replica", "space", None, None, None),
            P("replica", "space", None),
            P("replica", None),
            P("replica", None, None),
        ),
        out_specs=(
            P("replica", "space", None, None, None),
            P("replica", "space", None, None, None),
            P(),
            P(),
        ),
        check_vma=False,
    )
```

profile of v0, /device:TPU:2, one launch (start us, length us, event | category | flops | bytes accessed | tf_op | source)
XLA Modules:
  0.0 632.6 jit_solution(13846627901247388370)
XLA Ops:
  15.1 66.9 %all-gather.5.cloned.1.call-done = bf16[32,2,64,128]{3,2,1,0:T(8,128)(2,1)} async-done(((bf16[2,2,64,128]{3,2,1,0:T(8,128)(2,1)}), bf16[32,2,64,128]{3,2,1,0:T(8,128)(2,1)}) %all-gather.5.cloned.1.call-update) | async-done | bytes 1048592 | tf_op jit(solution)/shard_map/all_gather | solution.py:78
  82.0 1.8 gather_fusion.1
  83.8 1.5 gather_fusion.2
  85.3 1.5 gather_fusion
  86.8 1.8 gather_fusion.6
  88.6 1.4 gather_fusion.5
  90.0 1.5 gather_fusion.7
  92.0 61.9 %all-gather.7.cloned.1.call-done = bf16[32,2,64,128]{3,2,0,1:T(8,128)(2,1)} async-done(((bf16[2,2,64,128]{3,2,0,1:T(8,128)(2,1)}), bf16[32,2,64,128]{3,2,0,1:T(8,128)(2,1)}) %all-gather.7.cloned.1.call-update) | async-done | bytes 1048592 | tf_op jit(solution)/shard_map/all_gather | solution.py:79
  153.9 1.8 gather_fusion.4
  155.8 1.8 gather_fusion.3
  157.8 1.3 maximum_bitcast_fusion
  159.0 2.7 maximum_maximum_fusion
  161.7 1.8 copy.238
  163.5 1.7 pad.5.clone
  165.6 2.9 fusion.7
  168.6 6.8 %add_multiply_fusion = (f32[64,16,9,128]{3,1,2,0:T(8,128)S(1)}, f32[64,16,9,128]{3,1,2,0:T(8,128)S(1)}) fusion(f32[128]{0:T(128)S(1)} %copy-done.5, pred[16,9]{0,1:T(8,128)(4,1)S(1)} %copy-done.6, bf16[3,3,128,128]{3,2,1,0:T(8,128)(2,1)S(1)} %copy-done, bf16[66,2,8,11,128]{4,1,3,2,0:T(2,128)(2,1)S(1)} %fusion.7), kind=kOutput, calls=%fused_computation.20 | convolution fusion | flops 2729705472 | bytes 12706448 | tf_op jit(solution)/shard_map/conv_general_dilated | solution.py:83
  175.4 1.5 copy.198
  176.9 1.5 copy.201
  178.5 6.6 %convert_reduce_fusion = (f32[128]{0:T(128)S(1)}, bf16[2,64,64,128]{3,1,2,0:T(8,128)(2,1)S(1)}, bf16[1,2,64,64,128]{4,2,3,1,0:T(8,128)(2,1)}) fusion(f32[64,2,72,128]{3,0,2,1:T(8,128)S(1)} %bitcast.186, f32[2,64,64]{1,2,0:T(8,128)S(1)} %copy.199, bf16[1,2,64,64,128]{4,3,2,1,0:T(8,128)(2,1)S(1)} %copy-done.4, f32[64,2,72,128]{3,0,2,1:T(8,128)S(1)} %bitcast.185), kind=kLoop, calls=%fused_computation.31 | loop fusion | flops 8388480 | bytes 14713344 | tf_op jit(solution)/shard_map/reduce_sum | solution.py:119
  185.2 2.6 fusion.34
  187.7 2.8 fusion.37
  190.5 2.8 fusion.40
  193.3 1.4 copy.217
  194.6 2.8 fusion.43
  197.4 3.3 fusion.44
  200.8 2.5 fusion.45
  203.3 2.7 fusion.48
  206.0 2.7 fusion.51
  213.1 4.3 copy.226
  217.4 75.4 %psum.15 = f32[128]{0:T(128)S(1)} all-reduce(f32[128]{0:T(128)S(1)} %get-tuple-element.44), channel_id=1, replica_groups=mesh['space'=16,'replica'=16] {'space','replica'}, use_global_device_ids=true, to_apply=%region_5.6 | all-reduce | flops 128 | bytes 1024 | tf_op jit(solution)/shard_map/psum | solution.py:55
  293.3 167.6 %all-reduce.7.cloned.1.call-done = f32[1152,128]{1,0:T(8,128)} async-done(((f32[1152,128]{1,0:T(8,128)}), f32[1152,128]{1,0:T(8,128)}) %all-reduce.7.cloned.1.call-update) | async-done | bytes 589840 | tf_op jit(solution)/shard_map/psum | solution.py:55
  460.9 1.9 broadcast_multiply_fusion
  462.8 67.5 %all-gather.9.cloned.1.call-done = bf16[32,2,64,128]{3,2,1,0:T(8,128)(2,1)} async-done(((bf16[2,2,64,128]{3,2,1,0:T(8,128)(2,1)}), bf16[32,2,64,128]{3,2,1,0:T(8,128)(2,1)}) %all-gather.9.cloned.1.call-update) | async-done | bytes 1048592 | tf_op jit(solution)/shard_map/all_gather | solution.py:100
  530.3 1.5 gather_fusion.8
  531.8 1.5 gather_fusion.10
  533.2 1.8 gather_fusion.9
  535.0 1.8 gather_fusion.14
  537.1 64.5 %all-gather.11.cloned.1.call-done = bf16[32,2,64,128]{3,2,0,1:T(8,128)(2,1)} async-done(((bf16[2,2,64,128]{3,2,0,1:T(8,128)(2,1)}), bf16[32,2,64,128]{3,2,0,1:T(8,128)(2,1)}) %all-gather.11.cloned.1.call-update) | async-done | bytes 1048592 | tf_op jit(solution)/shard_map/all_gather | solution.py:101
  601.6 1.8 gather_fusion.11
  603.3 1.8 gather_fusion.12
  605.3 1.4 gather_fusion.13
  606.8 1.5 gather_fusion.15
  608.4 1.5 maximum_bitcast_fusion.1
  609.9 1.7 copy.239
  611.7 1.7 pad.7.clone
  613.7 2.7 fusion.8
  616.5 5.9 select_convert_fusion
  623.2 2.7 copy.227
  (83 shorter events, 15.4 us)
Async XLA Ops:
  7.2 161.4 %copy-start = (bf16[3,3,128,128]{3,2,1,0:T(8,128)(2,1)S(1)}, bf16[3,3,128,128]{3,2,1,0:T(8,128)(2,1)}, u32[]{:S(2)}) copy-start(bf16[3,3,128,128]{3,2,1,0:T(8,128)(2,1)} %param.8) | copy-start | bytes 884740
  7.2 150.6 %copy-start.1 = (bf16[1,2,64,64,128]{4,3,2,1,0:T(8,128)(2,1)S(1)}, bf16[1,2,64,64,128]{4,3,2,1,0:T(8,128)(2,1)}, u32[]{:S(2)}) copy-start(bf16[1,2,64,64,128]{4,3,2,1,0:T(8,128)(2,1)} %param.7) | copy-start | bytes 6291460
  7.2 74.8 %all-gather.5.cloned.1.call-start = ((), (), s32[]{:S(2)}) async-start(), calls=%async_computation | async-start | bytes 1114112 | tf_op jit(solution)/shard_map/all_gather | solution.py:78
  8.8 145.0 %all-gather.7.cloned.1.call-start = ((), (), s32[]{:S(2)}) async-start(), calls=%async_computation.1 | async-start | bytes 1114112 | tf_op jit(solution)/shard_map/all_gather | solution.py:79
  10.7 450.2 %all-reduce.7.cloned.1.call-start = ((), (), s32[]{:S(2)}) async-start(), calls=%async_computation.4 | async-start | bytes 1179648 | tf_op jit(solution)/shard_map/psum | solution.py:55
  165.6 3.0 copy-start.5
  165.6 3.0 copy-start.6
  176.9 1.6 copy-start.4
  185.1 20.9 %copy-start.2 = (bf16[2,64,64,128]{3,1,2,0:T(8,128)(2,1)}, bf16[2,64,64,128]{3,1,2,0:T(8,128)(2,1)S(1)}, u32[]{:S(2)}) copy-start(bf16[2,64,64,128]{3,1,2,0:T(8,128)(2,1)S(1)} %get-tuple-element.45) | copy-start | bytes 6291460
  209.5 1.8 copy-start.3
  210.5 319.8 %all-gather.9.cloned.1.call-start = ((), (), s32[]{:S(2)}) async-start(), calls=%async_computation.2 | async-start | bytes 1114112 | tf_op jit(solution)/shard_map/all_gather | solution.py:100
  212.3 389.3 %all-gather.11.cloned.1.call-start = ((), (), s32[]{:S(2)}) async-start(), calls=%async_computation.3 | async-start | bytes 1114112 | tf_op jit(solution)/shard_map/all_gather | solution.py:101
Sparse Core Ops, SparseCore 0:
  10.4 71.5 all-gather.4
  84.4 69.4 all-gather.6
  210.6 250.2 all-reduce.6
  462.7 67.5 all-gather.8
  532.1 69.4 all-gather.10
where the time goes:
time: 640 us; the launch traced here: 633 us
  waiting for transfers between devices  429 us (67%)
  blocking collectives  75.4 us (12%)
  local copies, waits for them, and re-layouts  50.4 us (8%)
  matrix products  35.7 us (6%)
  other arithmetic  27.8 us (4%)
  between operations  14.5 us (2%)
    psum x1, waiting for transfers between devices, reduce_grads(): flat, total_b = lax.psum((flat, local_b), ('space', 'replica'))  168 us
    psum x1, blocking collectives, reduce_grads(): flat, total_b = lax.psum((flat, local_b), ('space', 'replica'))  75.4 us
    all_gather x1, waiting for transfers between devices, local(): lax.all_gather(grad_rows, 'space', axis=0, tiled=True)  67.5 us
    all_gather x1, waiting for transfers between devices, local(): lax.all_gather(rows, 'space', axis=0, tiled=True)  66.9 us
    all_gather x1, waiting for transfers between devices, local(): lax.all_gather(grad_cols, 'space', axis=0, tiled=True)  64.5 us
    all_gather x1, waiting for transfers between devices, local(): lax.all_gather(cols, 'space', axis=0, tiled=True)  61.9 us
    dot_general x9, matrix products, local(): lax.dot_general(source, flat_grad, (((0,), (0,)), ((), ())), preferred_el...  22.9 us
    gather x8, local copies, waits for them, and re-layouts, face(): got = table[slot_of[direction], side]  14.3 us
  transfers between devices with their start and end apart: 5, of which 5 were waited for; matrix products, arithmetic and copies ran while one was open for 5% of the time, Pallas kernels for 0%

commit v1 on v0

v1 whole, which is shorter than its diff:
```python
import functools

import jax
import jax.numpy as jnp
from jax import lax
from jax.experimental import pallas as pl
from jax.experimental.pallas import tpu as pltpu
from jax.sharding import PartitionSpec as P

MESH = pl.DeviceIdType.MESH
BF = jnp.bfloat16
F32 = jnp.float32

NS = 16
NR = 16
NZ = 8
NP = 16
T = 2
H = 64
C = 128
PITCH = 80
WEST, FIRST, EAST = 7, 8, 72
HALF = 640
CH = HALF // NP
OFF = float(2**20)
PB = 4
DIRS = 4


def at80(row, off):
    return pl.multiple_of(row * PITCH, 8) + off


def kernel(
    holo, weight, bias, cot, tissue, owners, owners_s, neigh,
    feat, ingrad, wgrad, bgrad,
    hv, cv, fv, gv, iv, frame, x3, g3, w4, w4g, acc, bacc, drops, cfr, slots_v, slots_s,
    s1, r1, s2, r2, arb, arcv, half, brcv, csrc, crcv, dsrc, dall, erc,
    lsem, osem, ss1, rs1, ss2, rs2, sa, ra, sb, rb, sc, rc, sd, rd, se, re,
):
    sp = lax.axis_index("space")
    rp = lax.axis_index("replica")
    z, ylo = lax.div(sp, 2), lax.rem(sp, 2)
    core = lax.rem(rp, 2)
    plane = lax.div(rp, 4) * 4 + lax.rem(lax.div(rp, 2), 2) * 2 + ylo

    def plane_dev(p):
        return (z * 2 + lax.rem(p, 2), lax.div(p, 2) * 2 + core)

    def z_dev(k):
        return (k * 2 + ylo, rp)

    partner = (sp, rp + 1 - 2 * core)

    def load_h(t):
        return pltpu.make_async_copy(holo.at[t], hv.at[t], lsem.at[t])

    def load_c(t):
        return pltpu.make_async_copy(cot.at[t], cv.at[t], lsem.at[T + t])

    for t in range(T):
        load_h(t).start()
    for t in range(T):
        load_c(t).start()

    barrier = pltpu.get_barrier_semaphore()

    def greet(o, carry):
        pl.semaphore_signal(
            barrier, inc=1, device_id=(lax.rem(sp + o, NS), rp), device_id_type=MESH
        )
        pl.semaphore_signal(
            barrier, inc=1, device_id=plane_dev(lax.rem(plane + o, NP)), device_id_type=MESH
        )
        return carry

    lax.fori_loop(1, NS, greet, 0)
    pl.semaphore_signal(barrier, inc=1, device_id=partner, device_id_type=MESH)

    def copy1(ph, m, src):
        return pltpu.make_async_remote_copy(
            src_ref=s1.at[ph, m], dst_ref=r1.at[ph, src],
            send_sem=ss1.at[ph, m], recv_sem=rs1.at[ph, src],
            device_id=(m, rp), device_id_type=MESH,
        )

    def copy2(ph, j, src):
        return pltpu.make_async_remote_copy(
            src_ref=s2.at[ph, j], dst_ref=r2.at[ph, src],
            send_sem=ss2.at[ph, j], recv_sem=rs2.at[ph, src],
            device_id=(j, rp), device_id_type=MESH,
        )

    def over_space(fn):
        def step(o, carry):
            fn(lax.rem(sp + o, NS))
            return carry

        lax.fori_loop(1, NS, step, 0)

    def exchange_out(ph, tiles):
        for t in range(T):
            top = tiles[t, 0]
            bottom = tiles[t, H - 1]
            left = frame[t, pl.ds(PITCH + FIRST, H, stride=PITCH), :].astype(BF)
            right = frame[t, pl.ds(PITCH + FIRST + H - 1, H, stride=PITCH), :].astype(BF)
            for d, line in enumerate((bottom, top, right, left)):
                for q in range(4):
                    s1[ph, 4 * d + q, t] = line[16 * q : 16 * q + 16]
            for k, (y, x) in enumerate(((H - 1, H - 1), (H - 1, 0), (0, H - 1), (0, 0))):
                cfr[NS, pl.ds(t * 4 + k, 1), :] = frame[
                    t, pl.ds((y + 1) * PITCH + FIRST + x, 1), :
                ]
        block = cfr[NS].astype(BF)
        for m in range(NS):
            s1[ph, m, T] = block
        r1[ph, sp] = s1[ph, sp]

    def exchange_send1(ph):
        over_space(lambda m: copy1(ph, m, sp).start())

    def exchange_route(ph):
        over_space(lambda i: copy1(ph, i, i).wait_recv())
        mine = lax.div(sp, 4)

        def route(j, carry):
            for u in range(T):
                s = slots_s[mine, T * j + u]
                s2[ph, j, u] = r1[ph, lax.div(s, 2), lax.rem(s, 2)]
            return carry

        lax.fori_loop(0, NS, route, 0)
        over_space(lambda j: copy2(ph, j, sp).start())
        r2[ph, sp] = s2[ph, sp]

    def exchange_in(ph):
        cfr[NS] = jnp.zeros((16, C), F32)

        def widen(i, carry):
            cfr[i] = r1[ph, i, T].astype(F32)
            return carry

        lax.fori_loop(0, NS, widen, 0)
        over_space(lambda i: copy2(ph, i, i).wait_recv())
        for t in range(T):
            for k, (row, col) in enumerate(
                ((0, WEST), (0, EAST), (H + 1, WEST), (H + 1, EAST))
            ):
                s = slots_s[DIRS + k, T * sp + t]
                frame[t, pl.ds(row * PITCH + col, 1), :] = cfr[
                    lax.div(s, 2), pl.ds(lax.rem(s, 2) * 4 + k, 1), :
                ]
            for q in range(4):
                frame[t, pl.ds(FIRST + 16 * q, 16), :] = r2[ph, q, t].astype(F32)
                frame[t, pl.ds((H + 1) * PITCH + FIRST + 16 * q, 16), :] = r2[
                    ph, 4 + q, t
                ].astype(F32)
                for d, col in ((2, WEST), (3, EAST)):
                    frame[t, pl.ds((16 * q + 1) * PITCH + col, 16, stride=PITCH), :] = r2[
                        ph, 4 * d + q, t
                    ].astype(F32)

    def exchange_end(ph):
        over_space(lambda m: copy1(ph, m, sp).wait_send())
        over_space(lambda m: copy2(ph, m, sp).wait_send())

    for t in range(T):
        load_h(t).wait()

        def fill(y, carry):
            frame[t, pl.ds(at80(y + 1, FIRST), H), :] = hv[t, y].astype(F32)
            return carry

        lax.fori_loop(0, H, fill, 0)
    cfr[NS] = jnp.zeros((16, C), F32)
    exchange_out(0, hv)
    pl.semaphore_wait(barrier, 2 * (NS - 1) + 1)
    exchange_send1(0)

    own = jnp.broadcast_to(owners[...], (2 * DIRS, 2 * NS))
    near = jnp.full((2 * DIRS, 2 * NS), -1, jnp.int32)
    for tile in range(2 * NS):
        near = jnp.where(own == tile, neigh[:, tile : tile + 1], near)
    found = jnp.full((2 * DIRS, 2 * NS), 2 * NS, jnp.int32)
    for slot in range(2 * NS):
        found = jnp.where(near == owners_s[0, slot], slot, found)
    slots_v[:, 0 : 2 * NS] = found
    to_smem = pltpu.make_async_copy(slots_v, slots_s, lsem.at[2 * T])
    to_smem.start()

    zeros = jnp.zeros((C, C), BF)
    for r in range(4):
        for b in range(3):
            for q in range(2):
                a = r - q
                rows, cols = pl.ds((r * 3 + b) * C, C), pl.ds(q * C, C)
                if 0 <= a <= 2:
                    w4[rows, cols] = weight[a, b]
                    w4g[rows, cols] = weight[2 - a, 2 - b].astype(F32).T.astype(BF)
                else:
                    w4[rows, cols] = zeros
                    w4g[rows, cols] = zeros
    line = lax.broadcasted_iota(jnp.int32, (C, 2 * C), 0)
    lane = lax.broadcasted_iota(jnp.int32, (C, 2 * C), 1)
    w4[12 * C : 13 * C, :] = jnp.where((line < H) == (lane < C), -OFF, 0.0).astype(BF)
    bacc[...] = jnp.zeros_like(bacc)
    acc[...] = jnp.zeros_like(acc)
    for t in range(T):
        for p in range(H // 2):
            drops[t * (H // 2) + p : t * (H // 2) + p + 1, :] = (
                1 - tissue[t : t + 1, p * C : (p + 1) * C]
            ).astype(F32)
    for i in range(2):
        r1[i, NS] = jnp.zeros((3, 16, C), BF)
    to_smem.wait()

    exchange_route(0)
    exchange_in(0)

    def shifts(dst):
        for t in range(T):

            def step(y, carry):
                for b in range(3):
                    dst[t, y, :, b * C : (b + 1) * C] = frame[
                        t, pl.ds(at80(y, WEST + b), H), :
                    ].astype(BF)
                return carry

            lax.fori_loop(0, H + 2, step, 0)

    shifts(x3)
    for t in range(T):
        load_c(t).wait()

    nb = (H // 2) // PB
    bias2 = jnp.concatenate([bias[...], bias[...]], axis=1)
    eye = (
        lax.broadcasted_iota(jnp.int32, (H, C), 0)
        == lax.broadcasted_iota(jnp.int32, (H, C), 1) % H
    )

    def window(src, t, p):
        return jnp.concatenate([src[t, 2 * p + r] for r in range(4)], axis=1)

    def forward(i, carry):
        t, p0 = lax.div(i, nb), lax.rem(i, nb) * PB
        parts = []
        for k in range(PB):
            drop = jnp.where(eye, drops[pl.ds(t * (H // 2) + p0 + k, 1), :], 0.0).astype(BF)
            parts.append(jnp.concatenate([window(x3, t, p0 + k), drop], axis=1))
        pre = jnp.dot(
            jnp.concatenate(parts, axis=0), w4[...], preferred_element_type=F32
        ) + bias2
        sigma = 0.5 * jnp.tanh(0.5 * pre) + 0.5
        act = pre * sigma
        slope = sigma + act * (1.0 - sigma)
        total = jnp.zeros((8, C), F32)
        for k in range(PB):
            for q in range(2):
                y = 2 * (p0 + k) + q
                rows, cols = slice(k * H, (k + 1) * H), slice(q * C, (q + 1) * C)
                fv[t, y] = act[rows, cols].astype(BF)
                g = (cv[t, y].astype(F32) * slope[rows, cols]).astype(BF)
                gv[t, y] = g
                wide = g.astype(F32)
                frame[t, pl.ds(at80(y + 1, FIRST), H), :] = wide
                total = total + jnp.sum(wide.reshape(H // 8, 8, C), axis=0)
        bacc[...] += total
        return carry

    lax.fori_loop(0, T * nb, forward, 0)
    out_f = pltpu.make_async_copy(fv, feat, osem.at[0])
    out_f.start()

    exchange_out(1, gv)
    exchange_send1(1)

    WB = 8

    def weights(t):
        def step(i, carry):
            p0 = i * WB
            left = jnp.concatenate(
                [
                    jnp.concatenate(
                        [gv[t, 2 * (p0 + k) + q] for k in range(WB)], axis=0
                    ).astype(F32).T.astype(BF)
                    for q in range(2)
                ],
                axis=0,
            )
            right = jnp.concatenate([window(x3, t, p0 + k) for k in range(WB)], axis=0)
            acc[...] += jnp.dot(left, right, preferred_element_type=F32)
            return carry

        lax.fori_loop(0, (H // 2) // WB, step, 0)

    weights(0)
    exchange_route(1)
    weights(1)

    for tap in range(9):
        a, b = tap // 3, tap % 3
        lo = slice((a * 3 + b) * C, (a * 3 + b + 1) * C)
        hi = slice(((a + 1) * 3 + b) * C, ((a + 1) * 3 + b + 1) * C)
        block = (acc[0:C, lo] + acc[C : 2 * C, hi]).T
        if tap < 4:
            arb[0, tap * C : (tap + 1) * C] = block
        elif tap == 4:
            arb[0, 4 * C : 4 * C + H] = block[:H]
            arb[1, 0:H] = block[H:]
        else:
            arb[1, H + (tap - 5) * C : H + (tap - 4) * C] = block
    bsum = jnp.sum(bacc[...], axis=0, keepdims=True)
    first = lax.broadcasted_iota(jnp.int32, (HALF - 576, C), 0) == 0
    for i in range(2):
        arb[i, 576:HALF] = jnp.where(first, bsum, 0.0)

    copy_a = pltpu.make_async_remote_copy(
        src_ref=arb.at[1 - core], dst_ref=arcv, send_sem=sa, recv_sem=ra,
        device_id=partner, device_id_type=MESH,
    )
    copy_a.start()

    def chunk(p):
        return pl.ds(pl.multiple_of(p * CH, 8), CH)

    def copy_b(p, src):
        return pltpu.make_async_remote_copy(
            src_ref=half.at[chunk(p)], dst_ref=brcv.at[src],
            send_sem=sb.at[p], recv_sem=rb.at[src],
            device_id=plane_dev(p), device_id_type=MESH,
        )

    def copy_c(k, src):
        return pltpu.make_async_remote_copy(
            src_ref=csrc, dst_ref=crcv.at[src], send_sem=sc.at[k], recv_sem=rc.at[src],
            device_id=z_dev(k), device_id_type=MESH,
        )

    def copy_d(p, src):
        return pltpu.make_async_remote_copy(
            src_ref=dsrc, dst_ref=dall.at[chunk(src)], send_sem=sd.at[p], recv_sem=rd.at[src],
            device_id=plane_dev(p), device_id_type=MESH,
        )

    copy_e = pltpu.make_async_remote_copy(
        src_ref=dall, dst_ref=erc, send_sem=se, recv_sem=re,
        device_id=partner, device_id_type=MESH,
    )

    def over_plane(fn):
        def step(o, carry):
            fn(lax.rem(plane + o, NP))
            return carry

        lax.fori_loop(1, NP, step, 0)

    def over_z(fn):
        def step(o, carry):
            fn(lax.rem(z + o, NZ))
            return carry

        lax.fori_loop(1, NZ, step, 0)

    def stage_b():
        copy_a.wait_recv()
        half[...] = arb[core] + arcv[...]
        over_plane(lambda p: copy_b(p, plane).start())
        brcv[plane] = half[chunk(plane)]

    def stage_c():
        over_plane(lambda p: copy_b(p, p).wait_recv())
        total = brcv[0]
        for p in range(1, NP):
            total = total + brcv[p]
        csrc[...] = total
        over_z(lambda k: copy_c(k, z).start())
        crcv[z] = total

    def stage_d():
        over_z(lambda k: copy_c(k, k).wait_recv())
        total = crcv[0]
        for k in range(1, NZ):
            total = total + crcv[k]
        total = total * float(NS * NR * T * H * H) ** -0.5
        dsrc[...] = total
        over_plane(lambda p: copy_d(p, plane).start())
        dall[chunk(plane)] = total

    def stage_e():
        over_plane(lambda p: copy_d(p, p).wait_recv())
        copy_e.start()

    exchange_in(1)
    stage_b()
    shifts(g3)

    def backward(t):
        def step(i, carry):
            p0 = i * PB
            got = jnp.dot(
                jnp.concatenate([window(g3, t, p0 + k) for k in range(PB)], axis=0),
                w4g[...],
                preferred_element_type=F32,
            )
            for k in range(PB):
                for q in range(2):
                    iv[t, 2 * (p0 + k) + q] = got[
                        k * H : (k + 1) * H, q * C : (q + 1) * C
                    ].astype(BF)
            return carry

        lax.fori_loop(0, nb, step, 0)
        pltpu.make_async_copy(iv.at[t], ingrad.at[t], osem.at[1 + t]).start()

    stage_c()
    backward(0)
    stage_d()
    backward(1)
    stage_e()

    exchange_end(0)
    exchange_end(1)
    copy_a.wait_send()
    over_plane(lambda p: copy_b(p, plane).wait_send())
    over_z(lambda k: copy_c(k, z).wait_send())
    over_plane(lambda p: copy_d(p, plane).wait_send())
    out_f.wait()
    for t in range(T):
        pltpu.make_async_copy(iv.at[t], ingrad.at[t], osem.at[1 + t]).wait()
    copy_e.wait()
    rows_mine = pl.ds(pl.multiple_of(core * 576, 8), 576)
    rows_other = pl.ds(pl.multiple_of((1 - core) * 576, 8), 576)
    wgrad[rows_mine, :] = dall[0:576]
    wgrad[rows_other, :] = erc[0:576]
    bgrad[...] = dall[576:577]


def local(hologram, weight, conv_bias, cotangent, tissue, owners, neighbours):
    vmem = pl.BlockSpec(memory_space=pltpu.VMEM)
    smem = pl.BlockSpec(memory_space=pltpu.SMEM)
    hbm = pl.BlockSpec(memory_space=pl.ANY)
    tiles = jax.ShapeDtypeStruct((T, H, H, C), BF)
    dma = pltpu.SemaphoreType.DMA
    feat, ingrad, wgrad, bgrad = pl.pallas_call(
        kernel,
        out_shape=(
            tiles,
            tiles,
            jax.ShapeDtypeStruct((9 * C, C), F32),
            jax.ShapeDtypeStruct((1, C), F32),
        ),
        in_specs=[hbm, vmem, vmem, hbm, vmem, vmem, smem, vmem],
        out_specs=(hbm, hbm, vmem, vmem),
        scratch_shapes=[
            pltpu.VMEM((T, H, H, C), BF),
            pltpu.VMEM((T, H, H, C), BF),
            pltpu.VMEM((T, H, H, C), BF),
            pltpu.VMEM((T, H, H, C), BF),
            pltpu.VMEM((T, H, H, C), BF),
            pltpu.VMEM((T, (H + 2) * PITCH, C), F32),
            pltpu.VMEM((T, H + 2, H, 3 * C), BF),
            pltpu.VMEM((T, H + 2, H, 3 * C), BF),
            pltpu.VMEM((13 * C, 2 * C), BF),
            pltpu.VMEM((12 * C, 2 * C), BF),
            pltpu.VMEM((2 * C, 12 * C), F32),
            pltpu.VMEM((8, C), F32),
            pltpu.VMEM((T * H // 2, C), F32),
            pltpu.VMEM((NS + 1, 16, C), F32),
            pltpu.VMEM((8, C), jnp.int32),
            pltpu.SMEM((8, C), jnp.int32),
            pltpu.VMEM((2, NS, 3, 16, C), BF),
            pltpu.VMEM((2, NS + 1, 3, 16, C), BF),
            pltpu.VMEM((2, NS, T, 16, C), BF),
            pltpu.VMEM((2, NS, T, 16, C), BF),
            pltpu.VMEM((2, HALF, C), F32),
            pltpu.VMEM((HALF, C), F32),
            pltpu.VMEM((HALF, C), F32),
            pltpu.VMEM((NP, CH, C), F32),
            pltpu.VMEM((CH, C), F32),
            pltpu.VMEM((NZ, CH, C), F32),
            pltpu.VMEM((CH, C), F32),
            pltpu.VMEM((HALF, C), F32),
            pltpu.VMEM((HALF, C), F32),
            dma((2 * T + 1,)),
            dma((1 + T,)),
            dma((2, NS)), dma((2, NS)), dma((2, NS)), dma((2, NS)),
            dma, dma,
            dma((NP,)), dma((NP,)),
            dma((NZ,)), dma((NZ,)),
            dma((NP,)), dma((NP,)),
            dma, dma,
        ],
        compiler_params=pltpu.CompilerParams(
            collective_id=0, has_side_effects=True, vmem_limit_bytes=56 * 2**20
        ),
        cost_estimate=pl.CostEstimate(
            flops=7247757312, bytes_accessed=10 * 2**20, transcendentals=2**20
        ),
        name="unet_conv_step",
    )(
        hologram[0], weight, conv_bias[None], cotangent[0], tissue[0], owners, owners,
        neighbours[0],
    )
    return (
        feat[None], ingrad[None], wgrad.reshape(3, 3, C, C), bgrad.reshape(C)
    )


def solution(mesh):
    return jax.shard_map(
        local,
        mesh=mesh,
        in_specs=(
            P("replica", "space", None, None, None),
            P(),
            P(),
            P("replica", "space", None, None, None),
            P("replica", "space", None),
            P("replica", None),
            P("replica", None, None),
        ),
        out_specs=(
            P("replica", "space", None, None, None),
            P("replica", "space", None, None, None),
            P(),
            P(),
        ),
        check_vma=False,
    )
```

time: 640 us -> 78.6 us (0.12)
  the two profiles are of different devices: /device:TPU:2 before, /device:TPU:1 now
where the time goes in v1:
time: 78.6 us; the launch traced here: 78.4 us
  Pallas kernels  71.8 us (91%)
  local copies, waits for them, and re-layouts  6 us (8%)
    pallas_call x1, Pallas kernels, local(): pl.pallas_call(kernel, out_shape=(tiles, tiles, jax.ShapeDtypeStruct((9 *...  71.8 us
    unnamed x10, local copies, waits for them, and re-layouts  6 us

profile of v1, /device:TPU:1, one launch (start us, length us, event | category | flops | bytes accessed | tf_op | source)
XLA Modules:
  0.0 78.4 jit_solution(16307128351238931674)
XLA Ops:
  0.6 71.8 %unet_conv_step.1 = (bf16[2,64,64,128]{3,2,1,0:T(8,128)(2,1)}, bf16[2,64,64,128]{3,2,1,0:T(8,128)(2,1)}, f32[1152,128]{1,0:T(8,128)}, f32[1,128]{1,0:T(1,128)}) custom-call(bf16[2,64,64,128]{3,2,1,0:T(8,128)(2,1)} %bitcast.12, bf16[3,3,128,128]{3,2,1,0:T(8,128)(2,1)} %weight.1, f32[1,128]{1,0:T(1,128)} %bitcast.16, bf16[2,64,64,128]{3,2,1,0:T(8,128)(2,1)} %bitcast.13, ...), custom_call_target="tpu_custom_call" | custom-call | flops 7247757312 | bytes 10485760 | tf_op jit(solution)/shard_map/unet_conv_step/pallas_call | solution.py:447
  72.4 0.0 copy-start
  72.4 3.2 %copy.15 = bf16[1,2,64,64,128]{4,3,2,1,0:T(8,128)(2,1)} copy(bf16[1,2,64,64,128]{4,3,2,1,0:T(8,128)(2,1)} %bitcast.10) | data formatting | bytes 4194304
  75.6 0.0 copy-done
  75.7 0.0 copy-start.1
  75.7 0.0 copy-start.2
  75.7 1.3 %copy.16 = bf16[1,2,64,64,128]{4,3,2,1,0:T(8,128)(2,1)} copy(bf16[1,2,64,64,128]{4,3,2,1,0:T(8,128)(2,1)S(1)} %bitcast.9) | data formatting | bytes 4194304
  77.0 0.1 copy-done.1
  77.1 0.8 %copy.17 = f32[3,3,128,128]{3,2,1,0:T(8,128)} copy(f32[3,3,128,128]{3,2,1,0:T(8,128)S(1)} %bitcast.11) | data formatting | bytes 1179648
  77.9 0.0 copy-done.2
  77.9 0.5 copy.18
Async XLA Ops:
  72.4 3.2 %copy-start = (bf16[2,64,64,128]{3,2,1,0:T(8,128)(2,1)S(1)}, bf16[2,64,64,128]{3,2,1,0:T(8,128)(2,1)}, u32[]{:S(2)}) copy-start(bf16[2,64,64,128]{3,2,1,0:T(8,128)(2,1)} %get-tuple-element.9) | copy-start | bytes 6291460
  75.7 1.4 %copy-start.1 = (f32[1152,128]{1,0:T(8,128)S(1)}, f32[1152,128]{1,0:T(8,128)}, u32[]{:S(2)}) copy-start(f32[1152,128]{1,0:T(8,128)} %get-tuple-element.10) | copy-start | bytes 1769476
  75.7 2.3 %copy-start.2 = (f32[1,128]{1,0:T(1,128)S(1)}, f32[1,128]{1,0:T(1,128)}, u32[]{:S(2)}) copy-start(f32[1,128]{1,0:T(1,128)} %get-tuple-element.11) | copy-start | bytes 1540

commit v2 on v1

v2 whole, which is shorter than its diff:
```python
import functools

import jax
import jax.numpy as jnp
from jax import lax
from jax.experimental import pallas as pl
from jax.experimental.pallas import tpu as pltpu
from jax.sharding import PartitionSpec as P

MESH = pl.DeviceIdType.MESH
BF = jnp.bfloat16
F32 = jnp.float32

NS = 16
NR = 16
NZ = 8
NP = 16
T = 2
H = 64
C = 128
PITCH = 80
WEST, FIRST, EAST = 7, 8, 72
HALF = 640
CH = HALF // NP
OFF = float(2**20)
PB = 16
WB = 32
DIRS = 4


def at80(row, off):
    return pl.multiple_of(row * PITCH, 8) + off


def kernel(
    holo, weight, bias, cot, tissue, owners, owners_s, neigh,
    feat, ingrad, packed,
    hv, cv, fv, gv, iv, fh, fg, x3, g3, w4, w4g, w9, w9g, pb, acc, bacc, raw2, drops,
    cotb, fb, gb, cfr, slots_v, slots_s,
    s1, r1, s2, r2, arb, arcv, half, brcv, csrc, crcv, dsrc, dall, erc,
    lsem, osem, ss1, rs1, ss2, rs2, sa, ra, sb, rb, sc, rc, sd, rd, se, re,
):
    sp = lax.axis_index("space")
    rp = lax.axis_index("replica")
    z, ylo = lax.div(sp, 2), lax.rem(sp, 2)
    core = lax.rem(rp, 2)
    plane = lax.div(rp, 4) * 4 + lax.rem(lax.div(rp, 2), 2) * 2 + ylo

    def plane_dev(p):
        return (z * 2 + lax.rem(p, 2), lax.div(p, 2) * 2 + core)

    def z_dev(k):
        return (k * 2 + ylo, rp)

    partner = (sp, rp + 1 - 2 * core)

    def load_h(t):
        return pltpu.make_async_copy(holo.at[t], hv.at[t], lsem.at[t])

    def load_c(t):
        return pltpu.make_async_copy(cot.at[t], cv.at[t], lsem.at[T + t])

    for t in range(T):
        load_h(t).start()
    for t in range(T):
        load_c(t).start()

    barrier = pltpu.get_barrier_semaphore()

    def greet(o, carry):
        pl.semaphore_signal(
            barrier, inc=1, device_id=(lax.rem(sp + o, NS), rp), device_id_type=MESH
        )
        pl.semaphore_signal(
            barrier, inc=1, device_id=plane_dev(lax.rem(plane + o, NP)), device_id_type=MESH
        )
        return carry

    lax.fori_loop(1, NS, greet, 0)
    pl.semaphore_signal(barrier, inc=1, device_id=partner, device_id_type=MESH)

    def copy1(ph, m, src):
        return pltpu.make_async_remote_copy(
            src_ref=s1.at[ph, m], dst_ref=r1.at[ph, src],
            send_sem=ss1.at[ph, m], recv_sem=rs1.at[ph, src],
            device_id=(m, rp), device_id_type=MESH,
        )

    def copy2(ph, j, src):
        return pltpu.make_async_remote_copy(
            src_ref=s2.at[ph, j], dst_ref=r2.at[ph, src],
            send_sem=ss2.at[ph, j], recv_sem=rs2.at[ph, src],
            device_id=(j, rp), device_id_type=MESH,
        )

    def over_space(fn):
        def step(o, carry):
            fn(lax.rem(sp + o, NS))
            return carry

        lax.fori_loop(1, NS, step, 0)

    def exchange_out(ph, edges):
        for t in range(T):
            top, bottom, left, right = edges(t)
            for d, line in enumerate((bottom, top, right, left)):
                line = line.astype(BF)
                for q in range(4):
                    s1[ph, 4 * d + q, t] = line[16 * q : 16 * q + 16]
            for k, cell in enumerate((bottom[H - 1 :], bottom[:1], top[H - 1 :], top[:1])):
                cfr[NS, pl.ds(t * 4 + k, 1), :] = cell
        block = cfr[NS].astype(BF)
        for m in range(NS):
            s1[ph, m, T] = block
        r1[ph, sp] = s1[ph, sp]

    def exchange_send1(ph):
        over_space(lambda m: copy1(ph, m, sp).start())

    def exchange_route(ph):
        over_space(lambda i: copy1(ph, i, i).wait_recv())
        mine = lax.div(sp, 4)

        def route(j, carry):
            for u in range(T):
                s = slots_s[mine, T * j + u]
                s2[ph, j, u] = r1[ph, lax.div(s, 2), lax.rem(s, 2)]
            return carry

        lax.fori_loop(0, NS, route, 0)
        over_space(lambda j: copy2(ph, j, sp).start())
        r2[ph, sp] = s2[ph, sp]
        cfr[NS] = jnp.zeros((16, C), F32)

        def widen(i, carry):
            cfr[i] = r1[ph, i, T].astype(F32)
            return carry

        lax.fori_loop(0, NS, widen, 0)

    def exchange_in(ph, frame):
        for t in range(T):
            for k, (row, col) in enumerate(
                ((0, WEST), (0, EAST), (H + 1, WEST), (H + 1, EAST))
            ):
                s = slots_s[DIRS + k, T * sp + t]
                frame[t, pl.ds(row * PITCH + col, 1), :] = cfr[
                    lax.div(s, 2), pl.ds(lax.rem(s, 2) * 4 + k, 1), :
                ]
        over_space(lambda i: copy2(ph, i, i).wait_recv())
        for t in range(T):
            for q in range(4):
                frame[t, pl.ds(FIRST + 16 * q, 16), :] = r2[ph, q, t].astype(F32)
                frame[t, pl.ds((H + 1) * PITCH + FIRST + 16 * q, 16), :] = r2[
                    ph, 4 + q, t
                ].astype(F32)
                for d, col in ((2, WEST), (3, EAST)):
                    frame[t, pl.ds((16 * q + 1) * PITCH + col, 16, stride=PITCH), :] = r2[
                        ph, 4 * d + q, t
                    ].astype(F32)

    def exchange_end(ph):
        over_space(lambda m: copy1(ph, m, sp).wait_send())
        over_space(lambda m: copy2(ph, m, sp).wait_send())

    def column(x):
        return pl.ds(PITCH + FIRST + x, H, stride=PITCH)

    for t in range(T):
        load_h(t).wait()

        def fill(y, carry):
            fh[t, pl.ds(at80(y + 1, FIRST), H), :] = hv[t, y].astype(F32)
            return carry

        lax.fori_loop(0, H, fill, 0)
    cfr[NS] = jnp.zeros((16, C), F32)
    exchange_out(
        0,
        lambda t: (
            hv[t, 0].astype(F32), hv[t, H - 1].astype(F32),
            fh[t, column(0), :], fh[t, column(H - 1), :],
        ),
    )
    pl.semaphore_wait(barrier, 2 * (NS - 1) + 1)
    exchange_send1(0)

    own = jnp.broadcast_to(owners[...], (2 * DIRS, 2 * NS))
    near = jnp.full((2 * DIRS, 2 * NS), -1, jnp.int32)
    for tile in range(2 * NS):
        near = jnp.where(own == tile, neigh[:, tile : tile + 1], near)
    found = jnp.full((2 * DIRS, 2 * NS), 2 * NS, jnp.int32)
    for slot in range(2 * NS):
        found = jnp.where(near == owners_s[0, slot], slot, found)
    slots_v[:, 0 : 2 * NS] = found
    to_smem = pltpu.make_async_copy(slots_v, slots_s, lsem.at[2 * T])
    to_smem.start()

    zeros = jnp.zeros((C, C), BF)
    for r in range(4):
        for b in range(3):
            for q in range(2):
                a = r - q
                rows, cols = pl.ds((r * 3 + b) * C, C), pl.ds(q * C, C)
                if 0 <= a <= 2:
                    w4[rows, cols] = weight[a, b]
                else:
                    w4[rows, cols] = zeros
    line = lax.broadcasted_iota(jnp.int32, (C, 2 * C), 0)
    lane = lax.broadcasted_iota(jnp.int32, (C, 2 * C), 1)
    w4[12 * C : 13 * C, :] = jnp.where((line < H) == (lane < C), -OFF, 0.0).astype(BF)
    bacc[...] = jnp.zeros_like(bacc)
    acc[...] = jnp.zeros_like(acc)
    for i in range(2):
        r1[i, NS] = jnp.zeros((3, 16, C), BF)
    for t in range(T):
        for p in range(H // 2):
            got = (1 - tissue[t : t + 1, p * C : (p + 1) * C]).astype(F32)
            raw2[t, 2 * p : 2 * p + 1, :] = got
            raw2[t, 2 * p + 1 : 2 * p + 2, :] = got
            drops[t, p : p + 1, :] = got
    prow = lax.broadcasted_iota(jnp.int32, (H // 2, C), 0)
    plane_lane = lax.broadcasted_iota(jnp.int32, (H // 2, C), 1)
    outer = (
        (plane_lane % H == 0)
        | (plane_lane % H == H - 1)
        | ((prow == 0) & (plane_lane < H))
        | ((prow == H // 2 - 1) & (plane_lane >= H))
    )
    for t in range(T):
        drops[t] = jnp.where(outer, 1.0, drops[t])
    for frame in (fh, fg):
        for t in range(T):
            frame[t, 0:PITCH, :] = jnp.zeros((PITCH, C), F32)
            frame[t, (H + 1) * PITCH : (H + 2) * PITCH, :] = jnp.zeros((PITCH, C), F32)
            frame[t, column(-1), :] = jnp.zeros((H, C), F32)
            frame[t, column(H), :] = jnp.zeros((H, C), F32)
    to_smem.wait()

    def shifts(dst, frame, t):
        def step(y, carry):
            for b in range(3):
                dst[t, y, :, b * C : (b + 1) * C] = frame[
                    t, pl.ds(at80(y, WEST + b), H), :
                ].astype(BF)
            return carry

        lax.fori_loop(0, H + 2, step, 0, unroll=2)

    nb = (H // 2) // PB
    bias2 = jnp.concatenate([bias[...], bias[...]], axis=1)
    sub = lax.broadcasted_iota(jnp.int32, (H, C), 0)
    lanes = lax.broadcasted_iota(jnp.int32, (H, C), 1)
    eye = sub == lanes % H

    def window(src, t, p):
        return jnp.concatenate([src[t, 2 * p + r] for r in range(4)], axis=1)

    def activate(pre):
        sigma = 0.5 * jnp.tanh(0.5 * pre) + 0.5
        act = pre * sigma
        return act, sigma + act * (1.0 - sigma)

    def forward(t):
        def step(i, carry):
            p0 = i * PB
            parts = []
            for k in range(PB):
                drop = jnp.where(eye, drops[t, pl.ds(p0 + k, 1), :], 0.0).astype(BF)
                parts.append(jnp.concatenate([window(x3, t, p0 + k), drop], axis=1))
            pre = jnp.dot(
                jnp.concatenate(parts, axis=0), w4[...], preferred_element_type=F32
            ) + bias2
            act, slope = activate(pre)
            total = jnp.zeros((8, C), F32)
            for k in range(PB):
                for q in range(2):
                    y = 2 * (p0 + k) + q
                    rows, cols = slice(k * H, (k + 1) * H), slice(q * C, (q + 1) * C)
                    fv[t, y] = act[rows, cols].astype(BF)
                    wide = cv[t, y].astype(F32)
                    cotb[t, 2, pl.ds(y, 1), :] = wide[:1]
                    cotb[t, 3, pl.ds(y, 1), :] = wide[H - 1 :]
                    g = (wide * slope[rows, cols]).astype(BF)
                    gv[t, y] = g
                    wide = g.astype(F32)
                    fg[t, pl.ds(at80(y + 1, FIRST), H), :] = wide
                    total = total + jnp.sum(wide.reshape(H // 8, 8, C), axis=0)
            bacc[...] += total
            return carry

        lax.fori_loop(0, nb, step, 0)

    def weights(t):
        def step(i, carry):
            p0 = i * WB
            left = jnp.concatenate(
                [
                    jnp.concatenate(
                        [gv[t, 2 * (p0 + k) + q] for k in range(WB)], axis=0
                    ).astype(F32).T.astype(BF)
                    for q in range(2)
                ],
                axis=0,
            )
            right = jnp.concatenate([window(x3, t, p0 + k) for k in range(WB)], axis=0)
            acc[...] += jnp.dot(left, right, preferred_element_type=F32)
            return carry

        lax.fori_loop(0, (H // 2) // WB, step, 0)

    def backward(t):
        def step(i, carry):
            p0 = i * PB
            got = jnp.dot(
                jnp.concatenate([window(g3, t, p0 + k) for k in range(PB)], axis=0),
                w4g[...],
                preferred_element_type=F32,
            )
            for k in range(PB):
                for q in range(2):
                    iv[t, 2 * (p0 + k) + q] = got[
                        k * H : (k + 1) * H, q * C : (q + 1) * C
                    ].astype(BF)
            return carry

        lax.fori_loop(0, nb, step, 0)

    def patches(frame):
        for t in range(T):
            for side in range(4):
                rows = slice((t * 4 + side) * H, (t * 4 + side + 1) * H)
                y0 = H - 1 if side == 1 else 0
                x0 = H - 1 if side == 3 else 0
                stride = PITCH if side >= 2 else None
                for a in range(3):
                    for b in range(3):
                        got = frame[t, pl.ds((y0 + a) * PITCH + WEST + x0 + b, H, stride=stride), :]
                        tap = a * 3 + b
                        pb[rows, tap * C : (tap + 1) * C] = got.astype(BF)

    def put_columns(dst, src, t):
        low = lax.broadcasted_iota(jnp.int32, (16, C), 0) == 0
        high = lax.broadcasted_iota(jnp.int32, (16, C), 0) == 15

        def step(y, carry):
            first = dst[t, y, 0:16, :].astype(F32)
            dst[t, y, 0:16, :] = jnp.where(low, src[t, 2, pl.ds(y, 1), :], first).astype(BF)
            last = dst[t, y, H - 16 : H, :].astype(F32)
            dst[t, y, H - 16 : H, :] = jnp.where(
                high, src[t, 3, pl.ds(y, 1), :], last
            ).astype(BF)
            return carry

        lax.fori_loop(0, H, step, 0, unroll=4)

    def put_rows(dst, src, t):
        dst[t, 0] = src[t, 0].astype(BF)
        dst[t, H - 1] = src[t, 1].astype(BF)

    copy_a = pltpu.make_async_remote_copy(
        src_ref=arb.at[1 - core], dst_ref=arcv, send_sem=sa, recv_sem=ra,
        device_id=partner, device_id_type=MESH,
    )

    def chunk(p):
        return pl.ds(pl.multiple_of(p * CH, 8), CH)

    def copy_b(p, src):
        return pltpu.make_async_remote_copy(
            src_ref=half.at[chunk(p)], dst_ref=brcv.at[src],
            send_sem=sb.at[p], recv_sem=rb.at[src],
            device_id=plane_dev(p), device_id_type=MESH,
        )

    def copy_c(k, src):
        return pltpu.make_async_remote_copy(
            src_ref=csrc, dst_ref=crcv.at[src], send_sem=sc.at[k], recv_sem=rc.at[src],
            device_id=z_dev(k), device_id_type=MESH,
        )

    def copy_d(p, src):
        return pltpu.make_async_remote_copy(
            src_ref=dsrc, dst_ref=dall.at[chunk(src)], send_sem=sd.at[p], recv_sem=rd.at[src],
            device_id=plane_dev(p), device_id_type=MESH,
        )

    copy_e = pltpu.make_async_remote_copy(
        src_ref=dall, dst_ref=erc, send_sem=se, recv_sem=re,
        device_id=partner, device_id_type=MESH,
    )

    def over_plane(fn):
        def step(o, carry):
            fn(lax.rem(plane + o, NP))
            return carry

        lax.fori_loop(1, NP, step, 0)

    def over_z(fn):
        def step(o, carry):
            fn(lax.rem(z + o, NZ))
            return carry

        lax.fori_loop(1, NZ, step, 0)

    def stage_b():
        copy_a.wait_recv()
        half[...] = arb[core] + arcv[...]
        over_plane(lambda p: copy_b(p, plane).start())
        brcv[plane] = half[chunk(plane)]

    def stage_c():
        over_plane(lambda p: copy_b(p, p).wait_recv())
        total = brcv[0]
        for p in range(1, NP):
            total = total + brcv[p]
        csrc[...] = total
        over_z(lambda k: copy_c(k, z).start())
        crcv[z] = total

    def stage_d():
        over_z(lambda k: copy_c(k, k).wait_recv())
        total = crcv[0]
        for k in range(1, NZ):
            total = total + crcv[k]
        total = total * float(NS * NR * T * H * H) ** -0.5
        dsrc[...] = total
        over_plane(lambda p: copy_d(p, plane).start())
        dall[chunk(plane)] = total

    def stage_e():
        over_plane(lambda p: copy_d(p, p).wait_recv())
        copy_e.start()

    def put_gradient(tap, block, add):
        def put(i, lo, size, val):
            rows = slice(lo, lo + size)
            arb[i, rows] = arb[i, rows] + val if add else val

        if tap < 4:
            put(0, tap * C, C, block)
        elif tap == 4:
            put(0, 4 * C, H, block[:H])
            put(1, 0, H, block[H:])
        else:
            put(1, H + (tap - 5) * C, C, block)

    shifts(x3, fh, 0)
    for t in range(T):
        load_c(t).wait()
    forward(0)
    exchange_route(0)
    shifts(x3, fh, 1)
    forward(1)
    weights(0)
    weights(1)
    for tap in range(9):
        a, b = tap // 3, tap % 3
        w9[tap * C : (tap + 1) * C, :] = weight[a, b]
        lo = slice((a * 3 + b) * C, (a * 3 + b + 1) * C)
        hi = slice(((a + 1) * 3 + b) * C, ((a + 1) * 3 + b + 1) * C)
        put_gradient(tap, (acc[0:C, lo] + acc[C : 2 * C, hi]).T, False)
    w9[9 * C : 10 * C, :] = jnp.full((C, C), -OFF, BF)
    for t in range(T):
        cotb[t, 0] = cv[t, 0].astype(F32)
        cotb[t, 1] = cv[t, H - 1].astype(F32)
        for side, keep in enumerate(
            (
                jnp.where(lanes == sub, raw2[t, 0:1, :], 0.0),
                jnp.where(lanes == sub + H, raw2[t, H - 1 : H, :], 0.0),
                jnp.where(lanes == sub % 2 * H, raw2[t], 0.0),
                jnp.where(lanes == sub % 2 * H + H - 1, raw2[t], 0.0),
            )
        ):
            rows = slice((t * 4 + side) * H, (t * 4 + side + 1) * H)
            pb[rows, 9 * C : 10 * C] = keep.astype(BF)

    exchange_in(0, fh)
    patches(fh)
    pre = jnp.dot(pb[...], w9[...], preferred_element_type=F32) + bias[...]
    act, slope = activate(pre)
    fb[...] = act.reshape(T, 4, H, C)
    grads = (cotb[...].reshape(T * 4 * H, C) * slope).astype(BF).astype(F32)
    gb[...] = grads.reshape(T, 4, H, C)
    spot = lax.broadcasted_iota(jnp.int32, (T * 4 * H, C), 0)
    once = (spot % (4 * H) < 2 * H) | ((spot % H > 0) & (spot % H < H - 1))
    grads = jnp.where(once, grads, 0.0)
    outer_w = jnp.dot(
        grads.T.astype(BF), pb[:, 0 : 9 * C], preferred_element_type=F32
    )
    for tap in range(9):
        put_gradient(tap, outer_w[:, tap * C : (tap + 1) * C].T, True)
    bsum = jnp.sum(bacc[...], axis=0, keepdims=True) + jnp.sum(grads, axis=0, keepdims=True)
    first = lax.broadcasted_iota(jnp.int32, (HALF - 576, C), 0) == 0
    for i in range(2):
        arb[i, 576:HALF] = jnp.where(first, bsum, 0.0)
    copy_a.start()

    cfr[NS] = jnp.zeros((16, C), F32)
    exchange_out(1, lambda t: tuple(gb[t, side] for side in range(4)))
    exchange_send1(1)
    stage_b()

    for t in range(T):
        put_rows(fv, fb, t)
        put_columns(fv, fb, t)
        fg[t, pl.ds(PITCH + FIRST, H), :] = gb[t, 0]
        fg[t, pl.ds(H * PITCH + FIRST, H), :] = gb[t, 1]
        fg[t, column(0), :] = gb[t, 2]
        fg[t, column(H - 1), :] = gb[t, 3]
    out_f = pltpu.make_async_copy(fv, feat, osem.at[0])
    out_f.start()
    for r in range(4):
        for b in range(3):
            for q in range(2):
                a = r - q
                rows, cols = pl.ds((r * 3 + b) * C, C), pl.ds(q * C, C)
                if 0 <= a <= 2:
                    turned = weight[2 - a, 2 - b].astype(F32).T.astype(BF)
                    w4g[rows, cols] = turned
                    if q == 0:
                        w9g[(a * 3 + b) * C : (a * 3 + b + 1) * C, :] = turned
                else:
                    w4g[rows, cols] = zeros
    shifts(g3, fg, 0)
    shifts(g3, fg, 1)
    exchange_route(1)
    stage_c()
    backward(0)
    backward(1)
    stage_d()

    exchange_in(1, fg)
    patches(fg)
    got = jnp.dot(pb[:, 0 : 9 * C], w9g[...], preferred_element_type=F32)
    fb[...] = got.reshape(T, 4, H, C)
    out_i = []
    for t in range(T):
        put_rows(iv, fb, t)
        put_columns(iv, fb, t)
        out_i.append(pltpu.make_async_copy(iv.at[t], ingrad.at[t], osem.at[1 + t]))
        out_i[t].start()
    stage_e()

    exchange_end(0)
    exchange_end(1)
    copy_a.wait_send()
    over_plane(lambda p: copy_b(p, plane).wait_send())
    over_z(lambda k: copy_c(k, z).wait_send())
    over_plane(lambda p: copy_d(p, plane).wait_send())
    out_f.wait()
    for t in range(T):
        out_i[t].wait()
    copy_e.wait()
    rows_mine = pl.ds(pl.multiple_of(core * 576, 8), 576)
    rows_other = pl.ds(pl.multiple_of((1 - core) * 576, 8), 576)
    packed[rows_mine, :] = dall[0:576]
    packed[rows_other, :] = erc[0:576]
    packed[1152:1160, :] = dall[576:584]


def finish(feat, ingrad, packed, feat_out, ingrad_out, wgrad, bgrad, fv, iv, sem):
    ins = [pltpu.make_async_copy(feat, fv, sem.at[0]), pltpu.make_async_copy(ingrad, iv, sem.at[1])]
    outs = [
        pltpu.make_async_copy(fv, feat_out, sem.at[2]),
        pltpu.make_async_copy(iv, ingrad_out, sem.at[3]),
    ]
    for copy in ins:
        copy.start()
    wgrad[...] = packed[0 : 9 * C]
    bgrad[...] = packed[9 * C : 9 * C + 1]
    for one, other in zip(ins, outs):
        one.wait()
        other.start()
    for copy in outs:
        copy.wait()


def local(hologram, weight, conv_bias, cotangent, tissue, owners, neighbours):
    vmem = pl.BlockSpec(memory_space=pltpu.VMEM)
    smem = pl.BlockSpec(memory_space=pltpu.SMEM)
    hbm = pl.BlockSpec(memory_space=pl.ANY)
    tiles = jax.ShapeDtypeStruct((T, H, H, C), BF)
    dma = pltpu.SemaphoreType.DMA
    feat, ingrad, packed = pl.pallas_call(
        kernel,
        out_shape=(tiles, tiles, jax.ShapeDtypeStruct((9 * C + 8, C), F32)),
        in_specs=[hbm, vmem, vmem, hbm, vmem, vmem, smem, vmem],
        out_specs=(hbm, hbm, vmem),
        scratch_shapes=[
            pltpu.VMEM((T, H, H, C), BF),
            pltpu.VMEM((T, H, H, C), BF),
            pltpu.VMEM((T, H, H, C), BF),
            pltpu.VMEM((T, H, H, C), BF),
            pltpu.VMEM((T, H, H, C), BF),
            pltpu.VMEM((T, (H + 3) * PITCH, C), F32),
            pltpu.VMEM((T, (H + 3) * PITCH, C), F32),
            pltpu.VMEM((T, H + 2, H, 3 * C), BF),
            pltpu.VMEM((T, H + 2, H, 3 * C), BF),
            pltpu.VMEM((13 * C, 2 * C), BF),
            pltpu.VMEM((12 * C, 2 * C), BF),
            pltpu.VMEM((10 * C, C), BF),
            pltpu.VMEM((9 * C, C), BF),
            pltpu.VMEM((T * 4 * H, 10 * C), BF),
            pltpu.VMEM((2 * C, 12 * C), F32),
            pltpu.VMEM((8, C), F32),
            pltpu.VMEM((T, H, C), F32),
            pltpu.VMEM((T, H // 2, C), F32),
            pltpu.VMEM((T, 4, H, C), F32),
            pltpu.VMEM((T, 4, H, C), F32),
            pltpu.VMEM((T, 4, H, C), F32),
            pltpu.VMEM((NS + 1, 16, C), F32),
            pltpu.VMEM((8, C), jnp.int32),
            pltpu.SMEM((8, C), jnp.int32),
            pltpu.VMEM((2, NS, 3, 16, C), BF),
            pltpu.VMEM((2, NS + 1, 3, 16, C), BF),
            pltpu.VMEM((2, NS, T, 16, C), BF),
            pltpu.VMEM((2, NS, T, 16, C), BF),
            pltpu.VMEM((2, HALF, C), F32),
            pltpu.VMEM((HALF, C), F32),
            pltpu.VMEM((HALF, C), F32),
            pltpu.VMEM((NP, CH, C), F32),
            pltpu.VMEM((CH, C), F32),
            pltpu.VMEM((NZ, CH, C), F32),
            pltpu.VMEM((CH, C), F32),
            pltpu.VMEM((HALF, C), F32),
            pltpu.VMEM((HALF, C), F32),
            dma((2 * T + 1,)),
            dma((1 + T,)),
            dma((2, NS)), dma((2, NS)), dma((2, NS)), dma((2, NS)),
            dma, dma,
            dma((NP,)), dma((NP,)),
            dma((NZ,)), dma((NZ,)),
            dma((NP,)), dma((NP,)),
            dma, dma,
        ],
        compiler_params=pltpu.CompilerParams(
            collective_id=0, has_side_effects=True, vmem_limit_bytes=56 * 2**20
        ),
        cost_estimate=pl.CostEstimate(
            flops=7247757312, bytes_accessed=10 * 2**20, transcendentals=2**20
        ),
        name="unet_conv_step",
    )(
        hologram[0], weight, conv_bias[None], cotangent[0], tissue[0], owners, owners,
        neighbours[0],
    )
    feat, ingrad, wgrad, bgrad = pl.pallas_call(
        finish,
        out_shape=(
            tiles,
            tiles,
            jax.ShapeDtypeStruct((9 * C, C), F32),
            jax.ShapeDtypeStruct((1, C), F32),
        ),
        in_specs=[hbm, hbm, vmem],
        out_specs=(hbm, hbm, vmem, vmem),
        scratch_shapes=[
            pltpu.VMEM((T, H, H, C), BF), pltpu.VMEM((T, H, H, C), BF), dma((4,))
        ],
        compiler_params=pltpu.CompilerParams(vmem_limit_bytes=32 * 2**20),
        name="hand_over",
    )(feat, ingrad, packed)
    return (
        feat[None], ingrad[None], wgrad.reshape(3, 3, C, C), bgrad.reshape(C)
    )


def solution(mesh):
    return jax.shard_map(
        local,
        mesh=mesh,
        in_specs=(
            P("replica", "space", None, None, None),
            P(),
            P(),
            P("replica", "space", None, None, None),
            P("replica", "space", None),
            P("replica", None),
            P("replica", None, None),
        ),
        out_specs=(
            P("replica", "space", None, None, None),
            P("replica", "space", None, None, None),
            P(),
            P(),
        ),
        check_vma=False,
    )
```

time: 78.6 us -> 63.6 us (0.81)
  Pallas kernels: 71.8 us -> 58.5 us
  local copies, waits for them, and re-layouts: 6 us -> 4.24 us
    pallas_call x1, Pallas kernels: 71.8 us -> 55.3 us  [local(): pl.pallas_call(kernel, out_shape=(tiles, tiles, jax.ShapeDtypeStruct((9 *...]
    pallas_call x0 -> x1, Pallas kernels: none -> 3.18 us  [local(): pl.pallas_call(finish, out_shape=(tiles, tiles, jax.ShapeDtypeStruct((9 *...]
    unnamed x10 -> x6, local copies, waits for them, and re-layouts: 6 us -> 4.24 us
where the time goes in v2:
time: 63.6 us; the launch traced here: 63.4 us
  Pallas kernels  58.5 us (92%)
  local copies, waits for them, and re-layouts  4.24 us (7%)
  between operations  0.65 us (1%)
    pallas_call x1, Pallas kernels, local(): pl.pallas_call(kernel, out_shape=(tiles, tiles, jax.ShapeDtypeStruct((9 *...  55.3 us
    unnamed x6, local copies, waits for them, and re-layouts  4.24 us
    pallas_call x1, Pallas kernels, local(): pl.pallas_call(finish, out_shape=(tiles, tiles, jax.ShapeDtypeStruct((9 *...  3.18 us

profile of v2, /device:TPU:1, one launch (start us, length us, event | category | flops | bytes accessed | tf_op | source)
XLA Modules:
  0.0 63.4 jit_solution(16324338862342897196)
XLA Ops:
  0.6 55.3 %unet_conv_step.1 = (bf16[2,64,64,128]{3,2,1,0:T(8,128)(2,1)}, bf16[2,64,64,128]{3,2,1,0:T(8,128)(2,1)}, f32[1160,128]{1,0:T(8,128)}) custom-call(bf16[2,64,64,128]{3,2,1,0:T(8,128)(2,1)} %bitcast.9, bf16[3,3,128,128]{3,2,1,0:T(8,128)(2,1)} %weight.1, f32[1,128]{1,0:T(1,128)} %bitcast.16, bf16[2,64,64,128]{3,2,1,0:T(8,128)(2,1)} %bitcast.10, ...), custom_call_target="tpu_custom_call" | custom-call | flops 7247757312 | bytes 10485760 | tf_op jit(solution)/shard_map/unet_conv_step/pallas_call | solution.py:586
  56.0 0.0 copy-start
  56.0 1.6 %copy-done = bf16[2,64,64,128]{3,2,1,0:T(8,128)(2,1)S(1)} copy-done((bf16[2,64,64,128]{3,2,1,0:T(8,128)(2,1)S(1)}, bf16[2,64,64,128]{3,2,1,0:T(8,128)(2,1)}, u32[]{:S(2)}) %copy-start) | copy-done | bytes 2097176
  57.6 0.0 copy-start.1
  57.6 1.6 %copy-done.1 = bf16[2,64,64,128]{3,2,1,0:T(8,128)(2,1)S(1)} copy-done((bf16[2,64,64,128]{3,2,1,0:T(8,128)(2,1)S(1)}, bf16[2,64,64,128]{3,2,1,0:T(8,128)(2,1)}, u32[]{:S(2)}) %copy-start.1) | copy-done | bytes 2097176
  59.1 0.0 copy-start.2
  59.1 1.1 %copy-done.2 = f32[1160,128]{1,0:T(8,128)S(1)} copy-done((f32[1160,128]{1,0:T(8,128)S(1)}, f32[1160,128]{1,0:T(8,128)}, u32[]{:S(2)}) %copy-start.2) | copy-done | bytes 593944
  60.2 3.2 %hand_over.1 = (bf16[2,64,64,128]{3,2,1,0:T(8,128)(2,1)}, bf16[2,64,64,128]{3,2,1,0:T(8,128)(2,1)}, f32[1152,128]{1,0:T(8,128)}, f32[1,128]{1,0:T(1,128)}) custom-call(bf16[2,64,64,128]{3,2,1,0:T(8,128)(2,1)S(1)} %copy-done, bf16[2,64,64,128]{3,2,1,0:T(8,128)(2,1)S(1)} %copy-done.1, f32[1160,128]{1,0:T(8,128)S(1)} %copy-done.2), custom_call_target="tpu_custom_call" | custom-call | tf_op jit(solution)/shard_map/hand_over/pallas_call | solution.py:649
Async XLA Ops:
  56.0 1.6 %copy-start = (bf16[2,64,64,128]{3,2,1,0:T(8,128)(2,1)S(1)}, bf16[2,64,64,128]{3,2,1,0:T(8,128)(2,1)}, u32[]{:S(2)}) copy-start(bf16[2,64,64,128]{3,2,1,0:T(8,128)(2,1)} %get-tuple-element.11.feat) | copy-start | bytes 6291460
  57.6 1.6 %copy-start.1 = (bf16[2,64,64,128]{3,2,1,0:T(8,128)(2,1)S(1)}, bf16[2,64,64,128]{3,2,1,0:T(8,128)(2,1)}, u32[]{:S(2)}) copy-start(bf16[2,64,64,128]{3,2,1,0:T(8,128)(2,1)} %get-tuple-element.12.ingrad) | copy-start | bytes 6291460
  59.1 1.1 %copy-start.2 = (f32[1160,128]{1,0:T(8,128)S(1)}, f32[1160,128]{1,0:T(8,128)}, u32[]{:S(2)}) copy-start(f32[1160,128]{1,0:T(8,128)} %get-tuple-element.13.packed) | copy-start | bytes 1781764

commit v3 on v2

--- a/solution.py
+++ b/solution.py
@@ -20,8 +20,20 @@
 C = 128
 PITCH = 80
 WEST, FIRST, EAST = 7, 8, 72
-HALF = 640
-CH = HALF // NP
+CH = 48
+OWNERS = 13
+HALF = OWNERS * CH
+FAR_Z = (4, 3, 5, 2, 6, 1, 7)
+FAR_SPACE = sorted(
+    ((dz, dy) for dz in range(8) for dy in range(2) if dz or dy),
+    key=lambda d: -min(d[0], 8 - d[0]) - d[1],
+)
+FAR_PLANE = sorted(
+    ((dx, dy) for dx in range(4) for dy in range(4) if dx or dy),
+    key=lambda d: -min(d[0], 4 - d[0]) - min(d[1], 4 - d[1]),
+)
+CORNER_AT = (3, 0, 7, 4)
+CORNER_ROW = (15, 0, 15, 0)
 OFF = float(2**20)
 PB = 16
 WB = 32
@@ -33,12 +45,13 @@
 
 
 def kernel(
-    holo, weight, bias, cot, tissue, owners, owners_s, neigh,
-    feat, ingrad, packed,
-    hv, cv, fv, gv, iv, fh, fg, x3, g3, w4, w4g, w9, w9g, pb, acc, bacc, raw2, drops,
-    cotb, fb, gb, cfr, slots_v, slots_s,
-    s1, r1, s2, r2, arb, arcv, half, brcv, csrc, crcv, dsrc, dall, erc,
-    lsem, osem, ss1, rs1, ss2, rs2, sa, ra, sb, rb, sc, rc, sd, rd, se, re,
+    holo, weight_in, bias_in, cot, tissue_in, owners_in, neigh_in,
+    fv, iv, packed,
+    weight, bias, tissue, owners, owners_s, neigh,
+    hv, cv, gv, fh, fg, x3, w4, w4g, w9, w9g, pb, acc, bacc, raw2, drops,
+    cotb, fb, gb, slots_v, slots_s,
+    s1, r1a, r1b, s2, r2, s3, r3, arb, ah, arcv, half, brcv, csrc, crcv, dsrc, dall, erc,
+    lsem, ss1, rs1, ss2, rs2, ss3, rs3, sa, ra, sb, rb, sc, rc, sd, rd, se, re,
 ):
     sp = lax.axis_index("space")
     rp = lax.axis_index("replica")
@@ -53,6 +66,25 @@
         return (k * 2 + ylo, rp)
 
     partner = (sp, rp + 1 - 2 * core)
+    r1 = (r1a, r1b)
+
+    barrier = pltpu.get_barrier_semaphore()
+
+    def near_space(d):
+        return lax.rem(z + d[0], NZ) * 2 + lax.rem(ylo + d[1], 2)
+
+    def near_plane(d):
+        return lax.rem(lax.div(plane, 4) + d[0], 4) * 4 + lax.rem(lax.rem(plane, 4) + d[1], 4)
+
+    for d in FAR_SPACE:
+        pl.semaphore_signal(
+            barrier, inc=1, device_id=(near_space(d), rp), device_id_type=MESH
+        )
+    for d in FAR_PLANE:
+        pl.semaphore_signal(
+            barrier, inc=1, device_id=plane_dev(near_plane(d)), device_id_type=MESH
+        )
+    pl.semaphore_signal(barrier, inc=1, device_id=partner, device_id_type=MESH)
 
     def load_h(t):
         return pltpu.make_async_copy(holo.at[t], hv.at[t], lsem.at[t])
@@ -60,38 +92,60 @@
     def load_c(t):
         return pltpu.make_async_copy(cot.at[t], cv.at[t], lsem.at[T + t])
 
+    small = [
+        pltpu.make_async_copy(src, dst, lsem.at[2 * T + 1 + i])
+        for i, (src, dst) in enumerate(
+            (
+                (owners_in, owners), (owners_in, owners_s), (neigh_in, neigh),
+                (tissue_in, tissue), (bias_in, bias), (weight_in, weight),
+            )
+        )
+    ]
     for t in range(T):
         load_h(t).start()
+    for copy in small:
+        copy.start()
     for t in range(T):
         load_c(t).start()
 
-    barrier = pltpu.get_barrier_semaphore()
-
-    def greet(o, carry):
-        pl.semaphore_signal(
-            barrier, inc=1, device_id=(lax.rem(sp + o, NS), rp), device_id_type=MESH
-        )
-        pl.semaphore_signal(
-            barrier, inc=1, device_id=plane_dev(lax.rem(plane + o, NP)), device_id_type=MESH
-        )
-        return carry
-
-    lax.fori_loop(1, NS, greet, 0)
-    pl.semaphore_signal(barrier, inc=1, device_id=partner, device_id_type=MESH)
-
     def copy1(ph, m, src):
         return pltpu.make_async_remote_copy(
-            src_ref=s1.at[ph, m], dst_ref=r1.at[ph, src],
-            send_sem=ss1.at[ph, m], recv_sem=rs1.at[ph, src],
+            src_ref=s1.at[ph, m], dst_ref=r1[ph].at[src],
+            send_sem=ss1.at[ph], recv_sem=rs1.at[ph],
             device_id=(m, rp), device_id_type=MESH,
         )
 
     def copy2(ph, j, src):
         return pltpu.make_async_remote_copy(
             src_ref=s2.at[ph, j], dst_ref=r2.at[ph, src],
-            send_sem=ss2.at[ph, j], recv_sem=rs2.at[ph, src],
+            send_sem=ss2.at[ph], recv_sem=rs2.at[ph],
             device_id=(j, rp), device_id_type=MESH,
         )
+
+    def copy3(ph, j, k):
+        return pltpu.make_async_remote_copy(
+            src_ref=s3.at[ph, j], dst_ref=r3.at[ph, k],
+            send_sem=ss3.at[ph], recv_sem=rs3.at[ph, k],
+            device_id=(j, rp), device_id_type=MESH,
+        )
+
+    def step(src_ref, dst_ref, send_sem, recv_sem):
+        return pltpu.make_async_remote_copy(
+            src_ref=src_ref, dst_ref=dst_ref, send_sem=send_sem, recv_sem=recv_sem,
+            device_id=partner, device_id_type=MESH,
+        )
+
+    others = pl.ds(0, NS - 1)
+
+    def step1(ph):
+        return step(s1.at[ph, others], r1[ph].at[others], ss1.at[ph], rs1.at[ph])
+
+    def step2(ph):
+        return step(s2.at[ph, others], r2.at[ph, others], ss2.at[ph], rs2.at[ph])
+
+    def far_space(fn):
+        for d in FAR_SPACE:
+            fn(near_space(d))
 
     def over_space(fn):
         def step(o, carry):
@@ -107,47 +161,47 @@
                 line = line.astype(BF)
                 for q in range(4):
                     s1[ph, 4 * d + q, t] = line[16 * q : 16 * q + 16]
-            for k, cell in enumerate((bottom[H - 1 :], bottom[:1], top[H - 1 :], top[:1])):
-                cfr[NS, pl.ds(t * 4 + k, 1), :] = cell
-        block = cfr[NS].astype(BF)
-        for m in range(NS):
-            s1[ph, m, T] = block
-        r1[ph, sp] = s1[ph, sp]
+        r1[ph][sp] = s1[ph, sp]
 
     def exchange_send1(ph):
-        over_space(lambda m: copy1(ph, m, sp).start())
+        far_space(lambda m: copy1(ph, m, sp).start())
 
     def exchange_route(ph):
-        over_space(lambda i: copy1(ph, i, i).wait_recv())
+        step1(ph).wait_recv()
         mine = lax.div(sp, 4)
 
-        def route(j, carry):
+        def route(j):
             for u in range(T):
                 s = slots_s[mine, T * j + u]
-                s2[ph, j, u] = r1[ph, lax.div(s, 2), lax.rem(s, 2)]
-            return carry
-
-        lax.fori_loop(0, NS, route, 0)
-        over_space(lambda j: copy2(ph, j, sp).start())
+                s2[ph, j, u] = r1[ph][lax.div(s, 2), lax.rem(s, 2)]
+
+        def send(j):
+            route(j)
+            copy2(ph, j, sp).start()
+
+        far_space(send)
+        route(sp)
         r2[ph, sp] = s2[ph, sp]
-        cfr[NS] = jnp.zeros((16, C), F32)
-
-        def widen(i, carry):
-            cfr[i] = r1[ph, i, T].astype(F32)
-            return carry
-
-        lax.fori_loop(0, NS, widen, 0)
+        for k in range(DIRS):
+
+            @pl.when(sp == CORNER_AT[k])
+            def _():
+                def corner(j):
+                    for u in range(T):
+                        s = slots_s[DIRS + k, T * j + u]
+                        cells = r1[ph][lax.div(s, 2), lax.rem(s, 2)].astype(F32)
+                        s3[ph, j, u : u + 1] = cells[CORNER_ROW[k] : CORNER_ROW[k] + 1]
+
+                def give(j):
+                    corner(j)
+                    copy3(ph, j, k).start()
+
+                over_space(give)
+                corner(sp)
+                r3[ph, k] = s3[ph, sp]
 
     def exchange_in(ph, frame):
-        for t in range(T):
-            for k, (row, col) in enumerate(
-                ((0, WEST), (0, EAST), (H + 1, WEST), (H + 1, EAST))
-            ):
-                s = slots_s[DIRS + k, T * sp + t]
-                frame[t, pl.ds(row * PITCH + col, 1), :] = cfr[
-                    lax.div(s, 2), pl.ds(lax.rem(s, 2) * 4 + k, 1), :
-                ]
-        over_space(lambda i: copy2(ph, i, i).wait_recv())
+        step2(ph).wait_recv()
         for t in range(T):
             for q in range(4):
                 frame[t, pl.ds(FIRST + 16 * q, 16), :] = r2[ph, q, t].astype(F32)
@@ -158,10 +212,28 @@
                     frame[t, pl.ds((16 * q + 1) * PITCH + col, 16, stride=PITCH), :] = r2[
                         ph, 4 * d + q, t
                     ].astype(F32)
+        for k in range(DIRS):
+
+            @pl.when(sp != CORNER_AT[k])
+            def _():
+                copy3(ph, CORNER_AT[k], k).wait_recv()
+
+        for t in range(T):
+            for k, (row, col) in enumerate(
+                ((0, WEST), (0, EAST), (H + 1, WEST), (H + 1, EAST))
+            ):
+                frame[t, pl.ds(row * PITCH + col, 1), :] = r3[ph, k, t : t + 1]
 
     def exchange_end(ph):
-        over_space(lambda m: copy1(ph, m, sp).wait_send())
-        over_space(lambda m: copy2(ph, m, sp).wait_send())
+        step1(ph).wait_send()
+        step2(ph).wait_send()
+        for k in range(DIRS):
+
+            @pl.when(sp == CORNER_AT[k])
+            def _():
+                step(
+                    s3.at[ph, others], s3.at[ph, others], ss3.at[ph], rs3.at[ph, k]
+                ).wait_send()
 
     def column(x):
         return pl.ds(PITCH + FIRST + x, H, stride=PITCH)
@@ -174,7 +246,6 @@
             return carry
 
         lax.fori_loop(0, H, fill, 0)
-    cfr[NS] = jnp.zeros((16, C), F32)
     exchange_out(
         0,
         lambda t: (
@@ -184,6 +255,9 @@
     )
     pl.semaphore_wait(barrier, 2 * (NS - 1) + 1)
     exchange_send1(0)
+
+    for copy in small:
+        copy.wait()
 
     own = jnp.broadcast_to(owners[...], (2 * DIRS, 2 * NS))
     near = jnp.full((2 * DIRS, 2 * NS), -1, jnp.int32)
@@ -212,7 +286,7 @@
     bacc[...] = jnp.zeros_like(bacc)
     acc[...] = jnp.zeros_like(acc)
     for i in range(2):
-        r1[i, NS] = jnp.zeros((3, 16, C), BF)
+        r1[i][NS] = jnp.zeros((T, 16, C), BF)
     for t in range(T):
         for p in range(H // 2):
             got = (1 - tissue[t : t + 1, p * C : (p + 1) * C]).astype(F32)
@@ -313,7 +387,7 @@
         def step(i, carry):
             p0 = i * PB
             got = jnp.dot(
-                jnp.concatenate([window(g3, t, p0 + k) for k in range(PB)], axis=0),
+                jnp.concatenate([window(x3, t, p0 + k) for k in range(PB)], axis=0),
                 w4g[...],
                 preferred_element_type=F32,
             )
@@ -359,29 +433,29 @@
         dst[t, H - 1] = src[t, 1].astype(BF)
 
     copy_a = pltpu.make_async_remote_copy(
-        src_ref=arb.at[1 - core], dst_ref=arcv, send_sem=sa, recv_sem=ra,
+        src_ref=ah, dst_ref=arcv, send_sem=sa, recv_sem=ra,
         device_id=partner, device_id_type=MESH,
     )
 
     def chunk(p):
-        return pl.ds(pl.multiple_of(p * CH, 8), CH)
+        return pl.ds(pl.multiple_of(p * CH, 16), CH)
 
     def copy_b(p, src):
         return pltpu.make_async_remote_copy(
             src_ref=half.at[chunk(p)], dst_ref=brcv.at[src],
-            send_sem=sb.at[p], recv_sem=rb.at[src],
+            send_sem=sb, recv_sem=rb,
             device_id=plane_dev(p), device_id_type=MESH,
         )
 
     def copy_c(k, src):
         return pltpu.make_async_remote_copy(
-            src_ref=csrc, dst_ref=crcv.at[src], send_sem=sc.at[k], recv_sem=rc.at[src],
+            src_ref=csrc, dst_ref=crcv.at[src], send_sem=sc, recv_sem=rc,
             device_id=z_dev(k), device_id_type=MESH,
         )
 
     def copy_d(p, src):
         return pltpu.make_async_remote_copy(
-            src_ref=dsrc, dst_ref=dall.at[chunk(src)], send_sem=sd.at[p], recv_sem=rd.at[src],
+            src_ref=dsrc, dst_ref=dall.at[chunk(src)], send_sem=sd, recv_sem=rd,
             device_id=plane_dev(p), device_id_type=MESH,
         )
 
@@ -390,47 +464,67 @@
         device_id=partner, device_id_type=MESH,
     )
 
-    def over_plane(fn):
-        def step(o, carry):
-            fn(lax.rem(plane + o, NP))
-            return carry
-
-        lax.fori_loop(1, NP, step, 0)
-
-    def over_z(fn):
-        def step(o, carry):
-            fn(lax.rem(z + o, NZ))
-            return carry
-
-        lax.fori_loop(1, NZ, step, 0)
+    in_plane, in_ring = pl.ds(0, NP - 1), pl.ds(0, NZ - 1)
+
+    def step_b(rows):
+        return step(half.at[pl.ds(0, rows)], brcv.at[in_plane], sb, rb)
+
+    def step_c():
+        return step(crcv.at[in_ring], crcv.at[in_ring], sc, rc)
+
+    def step_d(rows):
+        return step(brcv.at[in_plane], dall.at[pl.ds(0, rows)], sd, rd)
+
+    owner = plane < OWNERS
+
+    def stage_a():
+        ah[...] = arb[1 - core].astype(BF)
+        copy_a.start()
 
     def stage_b():
         copy_a.wait_recv()
-        half[...] = arb[core] + arcv[...]
-        over_plane(lambda p: copy_b(p, plane).start())
-        brcv[plane] = half[chunk(plane)]
+        half[...] = (arb[core] + arcv[...].astype(F32)).astype(BF)
+        for d in FAR_PLANE:
+            p = near_plane(d)
+            pl.when(p < OWNERS)(lambda p=p: copy_b(p, plane).start())
+
+        @pl.when(owner)
+        def _():
+            brcv[plane] = half[chunk(plane)]
 
     def stage_c():
-        over_plane(lambda p: copy_b(p, p).wait_recv())
-        total = brcv[0]
-        for p in range(1, NP):
-            total = total + brcv[p]
-        csrc[...] = total
-        over_z(lambda k: copy_c(k, z).start())
-        crcv[z] = total
+        @pl.when(owner)
+        def _():
+            step_b(HALF).wait_recv()
+            total = brcv[0].astype(F32)
+            for p in range(1, NP):
+                total = total + brcv[p].astype(F32)
+            csrc[...] = total.astype(BF)
+            for d in FAR_Z:
+                copy_c(lax.rem(z + d, NZ), z).start()
+            crcv[z] = csrc[...]
 
     def stage_d():
-        over_z(lambda k: copy_c(k, k).wait_recv())
-        total = crcv[0]
-        for k in range(1, NZ):
-            total = total + crcv[k]
-        total = total * float(NS * NR * T * H * H) ** -0.5
-        dsrc[...] = total
-        over_plane(lambda p: copy_d(p, plane).start())
-        dall[chunk(plane)] = total
+        @pl.when(owner)
+        def _():
+            step_c().wait_recv()
+            total = crcv[0].astype(F32)
+            for k in range(1, NZ):
+                total = total + crcv[k].astype(F32)
+            dsrc[...] = (total * float(NS * NR * T * H * H) ** -0.5).astype(BF)
+            for d in FAR_PLANE:
+                copy_d(near_plane(d), plane).start()
+            dall[chunk(plane)] = dsrc[...]
 
     def stage_e():
-        over_plane(lambda p: copy_d(p, p).wait_recv())
+        @pl.when(owner)
+        def _():
+            step_d(HALF - CH).wait_recv()
+
+        @pl.when(jnp.logical_not(owner))
+        def _():
+            step_d(HALF).wait_recv()
+
         copy_e.start()
 
     def put_gradient(tap, block, add):
@@ -449,18 +543,10 @@
     shifts(x3, fh, 0)
     for t in range(T):
         load_c(t).wait()
-    forward(0)
-    exchange_route(0)
     shifts(x3, fh, 1)
-    forward(1)
-    weights(0)
-    weights(1)
     for tap in range(9):
         a, b = tap // 3, tap % 3
         w9[tap * C : (tap + 1) * C, :] = weight[a, b]
-        lo = slice((a * 3 + b) * C, (a * 3 + b + 1) * C)
-        hi = slice(((a + 1) * 3 + b) * C, ((a + 1) * 3 + b + 1) * C)
-        put_gradient(tap, (acc[0:C, lo] + acc[C : 2 * C, hi]).T, False)
     w9[9 * C : 10 * C, :] = jnp.full((C, C), -OFF, BF)
     for t in range(T):
         cotb[t, 0] = cv[t, 0].astype(F32)
@@ -476,6 +562,17 @@
             rows = slice((t * 4 + side) * H, (t * 4 + side + 1) * H)
             pb[rows, 9 * C : 10 * C] = keep.astype(BF)
 
+    forward(0)
+    exchange_route(0)
+    forward(1)
+    weights(0)
+    weights(1)
+    for tap in range(9):
+        a, b = tap // 3, tap % 3
+        lo = slice((a * 3 + b) * C, (a * 3 + b + 1) * C)
+        hi = slice(((a + 1) * 3 + b) * C, ((a + 1) * 3 + b + 1) * C)
+        put_gradient(tap, acc[0:C, lo] + acc[C : 2 * C, hi], False)
+
     exchange_in(0, fh)
     patches(fh)
     pre = jnp.dot(pb[...], w9[...], preferred_element_type=F32) + bias[...]
@@ -490,14 +587,13 @@
         grads.T.astype(BF), pb[:, 0 : 9 * C], preferred_element_type=F32
     )
     for tap in range(9):
-        put_gradient(tap, outer_w[:, tap * C : (tap + 1) * C].T, True)
+        put_gradient(tap, outer_w[:, tap * C : (tap + 1) * C], True)
     bsum = jnp.sum(bacc[...], axis=0, keepdims=True) + jnp.sum(grads, axis=0, keepdims=True)
     first = lax.broadcasted_iota(jnp.int32, (HALF - 576, C), 0) == 0
-    for i in range(2):
-        arb[i, 576:HALF] = jnp.where(first, bsum, 0.0)
-    copy_a.start()
-
-    cfr[NS] = jnp.zeros((16, C), F32)
+    arb[0, 576:HALF] = jnp.where(first, bsum, 0.0)
+    arb[1, 576:HALF] = jnp.zeros((HALF - 576, C), F32)
+    stage_a()
+
     exchange_out(1, lambda t: tuple(gb[t, side] for side in range(4)))
     exchange_send1(1)
     stage_b()
@@ -509,8 +605,6 @@
         fg[t, pl.ds(H * PITCH + FIRST, H), :] = gb[t, 1]
         fg[t, column(0), :] = gb[t, 2]
         fg[t, column(H - 1), :] = gb[t, 3]
-    out_f = pltpu.make_async_copy(fv, feat, osem.at[0])
-    out_f.start()
     for r in range(4):
         for b in range(3):
             for q in range(2):
@@ -523,8 +617,8 @@
                         w9g[(a * 3 + b) * C : (a * 3 + b + 1) * C, :] = turned
                 else:
                     w4g[rows, cols] = zeros
-    shifts(g3, fg, 0)
-    shifts(g3, fg, 1)
+    shifts(x3, fg, 0)
+    shifts(x3, fg, 1)
     exchange_route(1)
     stage_c()
     backward(0)
@@ -535,68 +629,81 @@
     patches(fg)
     got = jnp.dot(pb[:, 0 : 9 * C], w9g[...], preferred_element_type=F32)
     fb[...] = got.reshape(T, 4, H, C)
-    out_i = []
     for t in range(T):
         put_rows(iv, fb, t)
         put_columns(iv, fb, t)
-        out_i.append(pltpu.make_async_copy(iv.at[t], ingrad.at[t], osem.at[1 + t]))
-        out_i[t].start()
-    stage_e()
-
     exchange_end(0)
     exchange_end(1)
     copy_a.wait_send()
-    over_plane(lambda p: copy_b(p, plane).wait_send())
-    over_z(lambda k: copy_c(k, z).wait_send())
-    over_plane(lambda p: copy_d(p, plane).wait_send())
-    out_f.wait()
-    for t in range(T):
-        out_i[t].wait()
+
+    @pl.when(owner)
+    def _():
+        step_b(HALF - CH).wait_send()
+        step_c().wait_send()
+
+    @pl.when(jnp.logical_not(owner))
+    def _():
+        step_b(HALF).wait_send()
+
+    stage_e()
+
+    @pl.when(owner)
+    def _():
+        step_d(HALF).wait_send()
+
+    packed[core] = dall[...]
     copy_e.wait()
-    rows_mine = pl.ds(pl.multiple_of(core * 576, 8), 576)
-    rows_other = pl.ds(pl.multiple_of((1 - core) * 576, 8), 576)
-    packed[rows_mine, :] = dall[0:576]
-    packed[rows_other, :] = erc[0:576]
-    packed[1152:1160, :] = dall[576:584]
-
-
-def finish(feat, ingrad, packed, feat_out, ingrad_out, wgrad, bgrad, fv, iv, sem):
-    ins = [pltpu.make_async_copy(feat, fv, sem.at[0]), pltpu.make_async_copy(ingrad, iv, sem.at[1])]
-    outs = [
-        pltpu.make_async_copy(fv, feat_out, sem.at[2]),
-        pltpu.make_async_copy(iv, ingrad_out, sem.at[3]),
+    packed[1 - core] = erc[...]
+
+
+def finish(feat, ingrad, packed, feat_out, ingrad_out, wgrad_out, bgrad, wgrad, sem):
+    copies = [
+        pltpu.make_async_copy(feat, feat_out, sem.at[0]),
+        pltpu.make_async_copy(ingrad, ingrad_out, sem.at[1]),
+        pltpu.make_async_copy(wgrad, wgrad_out, sem.at[2]),
     ]
-    for copy in ins:
+    for copy in copies[:2]:
         copy.start()
-    wgrad[...] = packed[0 : 9 * C]
-    bgrad[...] = packed[9 * C : 9 * C + 1]
-    for one, other in zip(ins, outs):
-        one.wait()
-        other.start()
-    for copy in outs:
+    for tap in range(9):
+        if tap < 4:
+            block = packed[0, tap * C : (tap + 1) * C]
+        elif tap == 4:
+            block = jnp.concatenate([packed[0, 4 * C : 4 * C + H], packed[1, 0:H]], axis=0)
+        else:
+            block = packed[1, H + (tap - 5) * C : H + (tap - 4) * C]
+        wgrad[tap * C : (tap + 1) * C, :] = block.astype(F32).T
+    copies[2].start()
+    bgrad[...] = packed[0, 576 : 576 + 16].astype(F32)[0:1]
+    for copy in copies:
         copy.wait()
 
 
 def local(hologram, weight, conv_bias, cotangent, tissue, owners, neighbours):
     vmem = pl.BlockSpec(memory_space=pltpu.VMEM)
-    smem = pl.BlockSpec(memory_space=pltpu.SMEM)
-    hbm = pl.BlockSpec(memory_space=pl.ANY)
+    hbm = pl.BlockSpec(memory_space=pltpu.HBM)
     tiles = jax.ShapeDtypeStruct((T, H, H, C), BF)
     dma = pltpu.SemaphoreType.DMA
     feat, ingrad, packed = pl.pallas_call(
         kernel,
-        out_shape=(tiles, tiles, jax.ShapeDtypeStruct((9 * C + 8, C), F32)),
-        in_specs=[hbm, vmem, vmem, hbm, vmem, vmem, smem, vmem],
-        out_specs=(hbm, hbm, vmem),
-        scratch_shapes=[
+        out_shape=(
             pltpu.VMEM((T, H, H, C), BF),
             pltpu.VMEM((T, H, H, C), BF),
+            pltpu.VMEM((2, HALF, C), BF),
+        ),
+        in_specs=[hbm] * 7,
+        out_specs=(vmem, vmem, vmem),
+        scratch_shapes=[
+            pltpu.VMEM((3, 3, C, C), BF),
+            pltpu.VMEM((1, C), F32),
+            pltpu.VMEM((T, H * H), jnp.int32),
+            pltpu.VMEM((1, 2 * NS), jnp.int32),
+            pltpu.SMEM((1, 2 * NS), jnp.int32),
+            pltpu.VMEM((2 * DIRS, 2 * NS), jnp.int32),
             pltpu.VMEM((T, H, H, C), BF),
             pltpu.VMEM((T, H, H, C), BF),
             pltpu.VMEM((T, H, H, C), BF),
             pltpu.VMEM((T, (H + 3) * PITCH, C), F32),
             pltpu.VMEM((T, (H + 3) * PITCH, C), F32),
-            pltpu.VMEM((T, H + 2, H, 3 * C), BF),
             pltpu.VMEM((T, H + 2, H, 3 * C), BF),
             pltpu.VMEM((13 * C, 2 * C), BF),
             pltpu.VMEM((12 * C, 2 * C), BF),
@@ -610,41 +717,45 @@
             pltpu.VMEM((T, 4, H, C), F32),
             pltpu.VMEM((T, 4, H, C), F32),
             pltpu.VMEM((T, 4, H, C), F32),
-            pltpu.VMEM((NS + 1, 16, C), F32),
             pltpu.VMEM((8, C), jnp.int32),
             pltpu.SMEM((8, C), jnp.int32),
-            pltpu.VMEM((2, NS, 3, 16, C), BF),
-            pltpu.VMEM((2, NS + 1, 3, 16, C), BF),
+            pltpu.VMEM((2, NS, T, 16, C), BF),
+            pltpu.VMEM((NS + 1, T, 16, C), BF),
+            pltpu.VMEM((NS + 1, T, 16, C), BF),
             pltpu.VMEM((2, NS, T, 16, C), BF),
             pltpu.VMEM((2, NS, T, 16, C), BF),
+            pltpu.VMEM((2, NS, T, C), F32),
+            pltpu.VMEM((2, DIRS, T, C), F32),
             pltpu.VMEM((2, HALF, C), F32),
-            pltpu.VMEM((HALF, C), F32),
-            pltpu.VMEM((HALF, C), F32),
-            pltpu.VMEM((NP, CH, C), F32),
-            pltpu.VMEM((CH, C), F32),
-            pltpu.VMEM((NZ, CH, C), F32),
-            pltpu.VMEM((CH, C), F32),
-            pltpu.VMEM((HALF, C), F32),
-            pltpu.VMEM((HALF, C), F32),
-            dma((2 * T + 1,)),
-            dma((1 + T,)),
-            dma((2, NS)), dma((2, NS)), dma((2, NS)), dma((2, NS)),
-            dma, dma,
-            dma((NP,)), dma((NP,)),
-            dma((NZ,)), dma((NZ,)),
-            dma((NP,)), dma((NP,)),
-            dma, dma,
+            pltpu.VMEM((HALF, C), BF),
+            pltpu.VMEM((HALF, C), BF),
+            pltpu.VMEM((HALF, C), BF),
+            pltpu.VMEM((NP, CH, C), BF),
+            pltpu.VMEM((CH, C), BF),
+            pltpu.VMEM((NZ, CH, C), BF),
+            pltpu.VMEM((CH, C), BF),
+            pltpu.VMEM((HALF, C), BF),
+            pltpu.VMEM((HALF, C), BF),
+            dma((2 * T + 7,)),
+            dma((2,)), dma((2,)), dma((2,)), dma((2,)),
+            dma((2,)), dma((2, DIRS)),
+            dma, dma, dma, dma, dma, dma, dma, dma, dma, dma,
         ],
         compiler_params=pltpu.CompilerParams(
-            collective_id=0, has_side_effects=True, vmem_limit_bytes=56 * 2**20
+            collective_id=0, has_side_effects=True, vmem_limit_bytes=44 * 2**20
         ),
         cost_estimate=pl.CostEstimate(
             flops=7247757312, bytes_accessed=10 * 2**20, transcendentals=2**20
         ),
         name="unet_conv_step",
     )(
-        hologram[0], weight, conv_bias[None], cotangent[0], tissue[0], owners, owners,
-        neighbours[0],
+        *(
+            pltpu.with_memory_space_constraint(array, pltpu.HBM)
+            for array in (
+                hologram[0], weight, conv_bias[None], cotangent[0], tissue[0], owners,
+                neighbours[0],
+            )
+        )
     )
     feat, ingrad, wgrad, bgrad = pl.pallas_call(
         finish,
@@ -654,12 +765,12 @@
             jax.ShapeDtypeStruct((9 * C, C), F32),
             jax.ShapeDtypeStruct((1, C), F32),
         ),
-        in_specs=[hbm, hbm, vmem],
-        out_specs=(hbm, hbm, vmem, vmem),
+        in_specs=[vmem] * 3,
+        out_specs=(hbm, hbm, hbm, vmem),
         scratch_shapes=[
-            pltpu.VMEM((T, H, H, C), BF), pltpu.VMEM((T, H, H, C), BF), dma((4,))
+            pltpu.VMEM((9 * C, C), F32), dma((3,))
         ],
-        compiler_params=pltpu.CompilerParams(vmem_limit_bytes=32 * 2**20),
+        compiler_params=pltpu.CompilerParams(vmem_limit_bytes=10 * 2**20),
         name="hand_over",
     )(feat, ingrad, packed)
     return (

time: 63.6 us -> 47 us (0.74)
  Pallas kernels: 58.5 us -> 46.3 us
  local copies, waits for them, and re-layouts: 4.24 us -> 0 us
    pallas_call x1, Pallas kernels: 55.3 us -> 43.6 us  [local(): pl.pallas_call(kernel, out_shape=(pltpu.VMEM((T, H, H, C), BF), pltpu.VME...]
    unnamed x6 -> x0, local copies, waits for them, and re-layouts: 4.24 us -> none
where the time goes in v3:
time: 47 us; the launch traced here: 46.9 us
  Pallas kernels  46.3 us (99%)
  between operations  0.64 us (1%)
    pallas_call x1, Pallas kernels, local(): pl.pallas_call(kernel, out_shape=(pltpu.VMEM((T, H, H, C), BF), pltpu.VME...  43.6 us
    pallas_call x1, Pallas kernels, local(): pl.pallas_call(finish, out_shape=(tiles, tiles, jax.ShapeDtypeStruct((9 *...  2.75 us

profile of v3, /device:TPU:1, one launch (start us, length us, event | category | flops | bytes accessed | tf_op | source)
XLA Modules:
  0.0 46.9 jit_solution(2408673561352474094)
XLA Ops:
  0.6 43.6 %unet_conv_step.1 = (bf16[2,64,64,128]{3,2,1,0:T(8,128)(2,1)S(1)}, bf16[2,64,64,128]{3,2,1,0:T(8,128)(2,1)S(1)}, bf16[2,624,128]{2,1,0:T(8,128)(2,1)S(1)}) custom-call(bf16[2,64,64,128]{3,2,1,0:T(8,128)(2,1)} %bitcast.9, bf16[3,3,128,128]{3,2,1,0:T(8,128)(2,1)} %weight_in.1, f32[1,128]{1,0:T(1,128)} %bitcast.16, bf16[2,64,64,128]{3,2,1,0:T(8,128)(2,1)} %bitcast.10, ...), custom_call_target="tpu_custom_call" | custom-call | flops 7247757312 | bytes 10485760 | tf_op jit(solution)/shard_map/unet_conv_step/pallas_call | solution.py:686
  44.2 2.7 %hand_over.1 = (bf16[2,64,64,128]{3,2,1,0:T(8,128)(2,1)}, bf16[2,64,64,128]{3,2,1,0:T(8,128)(2,1)}, f32[1152,128]{1,0:T(8,128)}, f32[1,128]{1,0:T(1,128)}) custom-call(bf16[2,64,64,128]{3,2,1,0:T(8,128)(2,1)S(1)} %get-tuple-element.11.feat, bf16[2,64,64,128]{3,2,1,0:T(8,128)(2,1)S(1)} %get-tuple-element.12.ingrad, ...), custom_call_target="tpu_custom_call" | custom-call | tf_op jit(solution)/shard_map/hand_over/pallas_call | solution.py:760

commit v4 on v3

--- a/solution.py
+++ b/solution.py
@@ -23,7 +23,10 @@
 CH = 48
 OWNERS = 13
 HALF = OWNERS * CH
-FAR_Z = (4, 3, 5, 2, 6, 1, 7)
+FROM_ORIGIN_Z = (0, 1, 7, 2, 6, 3, 5, 4)
+FROM_ORIGIN = sorted(
+    range(16), key=lambda p: min(p // 4, 4 - p // 4) + min(p % 4, 4 - p % 4)
+)
 FAR_SPACE = sorted(
     ((dz, dy) for dz in range(8) for dy in range(2) if dz or dy),
     key=lambda d: -min(d[0], 8 - d[0]) - d[1],
@@ -36,7 +39,6 @@
 CORNER_ROW = (15, 0, 15, 0)
 OFF = float(2**20)
 PB = 16
-WB = 32
 DIRS = 4
 
 
@@ -101,10 +103,10 @@
             )
         )
     ]
-    for t in range(T):
-        load_h(t).start()
     for copy in small:
         copy.start()
+    for t in range(T):
+        load_h(t).start()
     for t in range(T):
         load_c(t).start()
 
@@ -237,24 +239,6 @@
 
     def column(x):
         return pl.ds(PITCH + FIRST + x, H, stride=PITCH)
-
-    for t in range(T):
-        load_h(t).wait()
-
-        def fill(y, carry):
-            fh[t, pl.ds(at80(y + 1, FIRST), H), :] = hv[t, y].astype(F32)
-            return carry
-
-        lax.fori_loop(0, H, fill, 0)
-    exchange_out(
-        0,
-        lambda t: (
-            hv[t, 0].astype(F32), hv[t, H - 1].astype(F32),
-            fh[t, column(0), :], fh[t, column(H - 1), :],
-        ),
-    )
-    pl.semaphore_wait(barrier, 2 * (NS - 1) + 1)
-    exchange_send1(0)
 
     for copy in small:
         copy.wait()
@@ -284,7 +268,6 @@
     lane = lax.broadcasted_iota(jnp.int32, (C, 2 * C), 1)
     w4[12 * C : 13 * C, :] = jnp.where((line < H) == (lane < C), -OFF, 0.0).astype(BF)
     bacc[...] = jnp.zeros_like(bacc)
-    acc[...] = jnp.zeros_like(acc)
     for i in range(2):
         r1[i][NS] = jnp.zeros((T, 16, C), BF)
     for t in range(T):
@@ -309,6 +292,24 @@
             frame[t, (H + 1) * PITCH : (H + 2) * PITCH, :] = jnp.zeros((PITCH, C), F32)
             frame[t, column(-1), :] = jnp.zeros((H, C), F32)
             frame[t, column(H), :] = jnp.zeros((H, C), F32)
+    for t in range(T):
+        load_h(t).wait()
+
+        def fill(y, carry):
+            fh[t, pl.ds(at80(y + 1, FIRST), H), :] = hv[t, y].astype(F32)
+            return carry
+
+        lax.fori_loop(0, H, fill, 0)
+    exchange_out(
+        0,
+        lambda t: (
+            hv[t, 0].astype(F32), hv[t, H - 1].astype(F32),
+            fh[t, column(0), :], fh[t, column(H - 1), :],
+        ),
+    )
+    pl.semaphore_wait(barrier, 2 * (NS - 1) + 1)
+    exchange_send1(0)
+
     to_smem.wait()
 
     def shifts(dst, frame, t):
@@ -363,25 +364,19 @@
             bacc[...] += total
             return carry
 
-        lax.fori_loop(0, nb, step, 0)
+        lax.fori_loop(0, nb, step, 0, unroll=True)
 
     def weights(t):
-        def step(i, carry):
-            p0 = i * WB
-            left = jnp.concatenate(
-                [
-                    jnp.concatenate(
-                        [gv[t, 2 * (p0 + k) + q] for k in range(WB)], axis=0
-                    ).astype(F32).T.astype(BF)
-                    for q in range(2)
-                ],
-                axis=0,
-            )
-            right = jnp.concatenate([window(x3, t, p0 + k) for k in range(WB)], axis=0)
-            acc[...] += jnp.dot(left, right, preferred_element_type=F32)
-            return carry
-
-        lax.fori_loop(0, (H // 2) // WB, step, 0)
+        left = jnp.concatenate(
+            [
+                jnp.concatenate([gv[t, 2 * p + q] for p in range(H // 2)], axis=0).T
+                for q in range(2)
+            ],
+            axis=0,
+        )
+        right = jnp.concatenate([window(x3, t, p) for p in range(H // 2)], axis=0)
+        got = jnp.dot(left, right, preferred_element_type=F32)
+        acc[...] = got if t == 0 else acc[...] + got
 
     def backward(t):
         def step(i, carry):
@@ -500,8 +495,8 @@
             for p in range(1, NP):
                 total = total + brcv[p].astype(F32)
             csrc[...] = total.astype(BF)
-            for d in FAR_Z:
-                copy_c(lax.rem(z + d, NZ), z).start()
+            for k in FROM_ORIGIN_Z:
+                pl.when(z != k)(lambda k=k: copy_c(k, z).start())
             crcv[z] = csrc[...]
 
     def stage_d():
@@ -512,8 +507,8 @@
             for k in range(1, NZ):
                 total = total + crcv[k].astype(F32)
             dsrc[...] = (total * float(NS * NR * T * H * H) ** -0.5).astype(BF)
-            for d in FAR_PLANE:
-                copy_d(near_plane(d), plane).start()
+            for p in FROM_ORIGIN:
+                pl.when(plane != p)(lambda p=p: copy_d(p, plane).start())
             dall[chunk(plane)] = dsrc[...]
 
     def stage_e():

time: 47 us -> 46.7 us (level)
  no operation moved by 1% of the time
where the time goes in v4:
time: 46.7 us; the launch traced here: 46.6 us
  Pallas kernels  46 us (99%)
  between operations  0.64 us (1%)
    pallas_call x1, Pallas kernels, local(): pl.pallas_call(kernel, out_shape=(pltpu.VMEM((T, H, H, C), BF), pltpu.VME...  43.2 us
    pallas_call x1, Pallas kernels, local(): pl.pallas_call(finish, out_shape=(tiles, tiles, jax.ShapeDtypeStruct((9 *...  2.75 us

profile of v4, /device:TPU:1, one launch (start us, length us, event | category | flops | bytes accessed | tf_op | source)
XLA Modules:
  0.0 46.6 jit_solution(14711042443778019778)
XLA Ops:
  0.6 43.2 %unet_conv_step.1 = (bf16[2,64,64,128]{3,2,1,0:T(8,128)(2,1)S(1)}, bf16[2,64,64,128]{3,2,1,0:T(8,128)(2,1)S(1)}, bf16[2,624,128]{2,1,0:T(8,128)(2,1)S(1)}) custom-call(bf16[2,64,64,128]{3,2,1,0:T(8,128)(2,1)} %bitcast.9, bf16[3,3,128,128]{3,2,1,0:T(8,128)(2,1)} %weight_in.1, f32[1,128]{1,0:T(1,128)} %bitcast.16, bf16[2,64,64,128]{3,2,1,0:T(8,128)(2,1)} %bitcast.10, ...), custom_call_target="tpu_custom_call" | custom-call | flops 7247757312 | bytes 10485760 | tf_op jit(solution)/shard_map/unet_conv_step/pallas_call | solution.py:681
  43.9 2.7 %hand_over.1 = (bf16[2,64,64,128]{3,2,1,0:T(8,128)(2,1)}, bf16[2,64,64,128]{3,2,1,0:T(8,128)(2,1)}, f32[1152,128]{1,0:T(8,128)}, f32[1,128]{1,0:T(1,128)}) custom-call(bf16[2,64,64,128]{3,2,1,0:T(8,128)(2,1)S(1)} %get-tuple-element.11.feat, bf16[2,64,64,128]{3,2,1,0:T(8,128)(2,1)S(1)} %get-tuple-element.12.ingrad, ...), custom_call_target="tpu_custom_call" | custom-call | tf_op jit(solution)/shard_map/hand_over/pallas_call | solution.py:755
